TPU v7x, 256 devices: a whole 4x4x8 slice. The times are simulated.
256 devices in a mesh: pipe: 4 (over y), dp: 32 (over z, x), tensor: 2 (over core).
Axes of the slice: x: 4, y: 4, z: 8, core: 2. Of those that a mesh axis runs over, the one named last changes fastest.
Arguments:
- llm_grad: bfloat16 [4, 1024, 1664], P(None, 'dp'), may hold values from -6 to 6
- slot_row: int32 [4, 32, 32], P(None, 'dp'), may hold values from 0 to 31, each once within a row
- counts: int32 [32, 4], P('dp'), may hold values from 8 to 32, as said below
- saved_in: bfloat16 [4, 4, 1024, 1664], P('pipe', None, 'dp'), may hold values from -6 to 6
- saved_pre: bfloat16 [4, 4, 1024, 6400], P('pipe', None, 'dp', 'tensor'), may hold values from -6 to 6
- weights: bfloat16 [4, 1664, 6400], P('pipe', 'dp', 'tensor'), may hold values from -0.15625 to 0.15625
- channel_scale: float32 [4, 1664], P('pipe'), may hold values from 0.25 to 2
Outputs:
- weight_grad: bfloat16 [4, 1664, 6400], P('pipe', 'dp', 'tensor')
- section_grad: bfloat16 [4, 4, 1024, 1664], P('pipe', None, 'dp')
Inputs may be any that keep to these rules, and one draw needn't show every extreme that they name: For each micro-batch and rank, slot_row lists every row of the rank once. `counts`: both ends of the range occur in every draw.
All inputs are finite; a program needn't handle non-finite values.
Results may differ from a plain program's by a relative error of at most 0.023.
Values may be sent and summed in bfloat16 or wider, within the bound.
A program may use at most 128 MiB of HBM per device.

v0:
```python
import jax
import jax.numpy as jnp
from jax import lax
from jax.sharding import PartitionSpec as P

norm_eps = 1e-06
root_half = 0.7071067811865476
inv_root_two_pi = 0.3989422804014327


def shortened(value):

    def short(part):
        return part.astype(jnp.bfloat16) if part.dtype == jnp.float32 else part

    return jax.tree.map(short, value)


def shifted(block, axis, distance):
    devices = range(lax.axis_size(axis))
    route = [(i - distance, i) for i in devices if i - distance in devices]
    return lax.ppermute(block, axis, route)


def gelu_parts(pre_act):
    normal_cdf = 0.5 * (1.0 + jax.scipy.special.erf(pre_act * root_half))
    density = jnp.exp(-0.5 * pre_act * pre_act) * inv_root_two_pi
    return (pre_act * normal_cdf, normal_cdf + pre_act * density)


def local_top(llm_grad, slot_row, counts):
    row_count = llm_grad.shape[1]
    slot_ids = jnp.arange(row_count, dtype=jnp.int32)
    kept_mask = slot_ids[None, :] < counts[:, None]
    source = jnp.where(kept_mask[..., None], llm_grad, jnp.zeros_like(llm_grad))
    onehot = (slot_row[:, :, None] == slot_ids[None, None, :]).astype(jnp.bfloat16)
    placed = jnp.einsum("mjr,mjd->mrd", onehot, source, preferred_element_type=jnp.float32)
    return placed.astype(jnp.bfloat16)


def norm_back(incoming, dnorm, unit_rows, inv_std, channel_gain):
    scaled_back = dnorm * channel_gain
    back = inv_std * (
        scaled_back
        - jnp.mean(scaled_back, axis=-1, keepdims=True)
        - unit_rows * jnp.mean(scaled_back * unit_rows, axis=-1, keepdims=True)
    )
    return (incoming.astype(jnp.float32) + back).astype(jnp.bfloat16)


def add_term(grad_total, left_side, right_side):
    return grad_total + lax.dot_general(
        left_side, right_side, (((0,), (0,)), ((), ())), preferred_element_type=jnp.float32
    )


def keep_total(grad_total, left_side, right_side):
    return grad_total


def body(llm_grad, slot_row, counts, saved_in, saved_pre, weights, channel_scale):
    sections = lax.axis_size("pipe")
    section_index = lax.axis_index("pipe")
    micro_count = llm_grad.shape[0]
    row_count = llm_grad.shape[1]
    model_width = llm_grad.shape[2]
    hidden = saved_pre.shape[3]
    is_up = section_index % 2 == 0
    is_top = section_index == sections - 1
    full_weight = lax.all_gather(weights[0], "dp", axis=0, tiled=True)
    channel_gain = channel_scale[0]
    top_grad = local_top(llm_grad, slot_row[:, 0], counts[0])
    zero_wide = jnp.zeros((row_count, model_width), jnp.float32)
    zero_narrow = jnp.zeros((row_count, model_width), jnp.bfloat16)
    zero_hidden = jnp.zeros((row_count, hidden), jnp.bfloat16)

    def spare_work(incoming, hidden_in, inputs, pre_act):
        return (zero_wide, zero_hidden, zero_narrow, zero_hidden)

    def down_work(incoming, hidden_in, inputs, pre_act):
        scaled = (incoming.astype(jnp.float32) * channel_gain).astype(jnp.bfloat16)
        hidden_grad = jnp.dot(scaled, full_weight, preferred_element_type=jnp.float32).astype(
            jnp.bfloat16
        )
        activated = gelu_parts(pre_act.astype(jnp.float32))[0].astype(jnp.bfloat16)
        return (zero_wide, hidden_grad, scaled, activated)

    def up_work(incoming, hidden_in, inputs, pre_act):
        act_grad = (
            hidden_in.astype(jnp.float32) * gelu_parts(pre_act.astype(jnp.float32))[1]
        ).astype(jnp.bfloat16)
        values = inputs.astype(jnp.float32)
        center = values - jnp.mean(values, axis=-1, keepdims=True)
        inv_std = lax.rsqrt(jnp.mean(center * center, axis=-1, keepdims=True) + norm_eps)
        normed = (center * inv_std * channel_gain).astype(jnp.bfloat16)
        partial_value = lax.dot_general(
            act_grad, full_weight, (((1,), (1,)), ((), ())), preferred_element_type=jnp.float32
        )
        return (partial_value, zero_hidden, normed, act_grad)

    def advance(loop_state, tick_index):
        grad_store, out_buffer, recv_hidden, recv_res = loop_state
        micro_index = tick_index - (sections - 1 - section_index)
        is_valid = (micro_index >= 0) & (micro_index < micro_count)
        micro_safe = jnp.clip(micro_index, 0, micro_count - 1)
        incoming = jnp.where(is_top, top_grad[micro_safe], recv_res)
        inputs = saved_in[0, micro_safe]
        pre_act = saved_pre[0, micro_safe]
        branch = jnp.where(is_valid, jnp.where(is_up, 2, 1), 0).astype(jnp.int32)
        partial_value, hidden_out, left_side, right_side = lax.switch(
            branch, [spare_work, down_work, up_work], incoming, recv_hidden, inputs, pre_act
        )
        values = inputs.astype(jnp.float32)
        center = values - jnp.mean(values, axis=-1, keepdims=True)
        inv_std = lax.rsqrt(jnp.mean(center * center, axis=-1, keepdims=True) + norm_eps)
        unit_rows = center * inv_std
        summed = jax.tree.map(
            lambda part: part.astype(jnp.float32), lax.psum(shortened(partial_value), "tensor")
        )
        back_out = norm_back(incoming, summed, unit_rows, inv_std, channel_gain)
        outgoing = jnp.where(is_up, back_out, incoming)
        write_at = jnp.where(is_valid, micro_safe, micro_count)
        out_buffer = lax.dynamic_update_index_in_dim(out_buffer, outgoing, write_at, 0)
        grad_store = lax.cond(is_valid, add_term, keep_total, grad_store, left_side, right_side)
        recv_hidden, recv_res = (
            shifted(shortened(hidden_out), "pipe", -1).astype(hidden_out.dtype),
            shifted(outgoing, "pipe", -1),
        )
        return ((grad_store, out_buffer, recv_hidden, recv_res), None)

    grad_store = jnp.zeros((model_width, hidden), jnp.float32)
    out_buffer = jnp.zeros((micro_count + 1, row_count, model_width), jnp.bfloat16)
    tick_count = micro_count + sections - 1
    loop_state = (grad_store, out_buffer, zero_hidden, zero_narrow)
    loop_state, unused = lax.scan(advance, loop_state, jnp.arange(tick_count, dtype=jnp.int32))
    grad_store, out_buffer, recv_hidden, recv_res = loop_state
    weight_out = lax.psum_scatter(
        grad_store.astype(jnp.bfloat16), "dp", scatter_dimension=0, tiled=True
    )
    return (weight_out[None], out_buffer[:micro_count][None])


def solution(mesh):
    in_specs = (
        P(None, "dp", None),
        P(None, "dp", None),
        P("dp", None),
        P("pipe", None, "dp", None),
        P("pipe", None, "dp", "tensor"),
        P("pipe", "dp", "tensor"),
        P("pipe", None),
    )
    out_specs = (P("pipe", "dp", "tensor"), P("pipe", None, "dp", None))
    return jax.shard_map(body, mesh=mesh, in_specs=in_specs, out_specs=out_specs, check_vma=False)
```

profile of v0, /device:TPU:160, one launch (start us, length us, event | category | flops | bytes accessed | tf_op | source)
XLA Modules:
  0.0 917.6 jit_solution(5709121995667591268)
XLA Ops:
  11.7 160.9 %all-gather.3.cloned.1.call-done = bf16[1,1664,3200]{2,0,1:T(2,128)(2,1)} async-done(((bf16[1,52,3200]{2,0,1:T(2,128)(2,1)}), bf16[1,1664,3200]{2,0,1:T(2,128)(2,1)}) %all-gather.3.cloned.1.call-update) | async-done | bytes 10649616 | tf_op jit(solution)/shard_map/all_gather | solution.py:70
  172.6 15.3 %copy.13 = bf16[1,1664,3200]{2,1,0:T(8,128)(2,1)} copy(bf16[1,1664,3200]{2,0,1:T(2,128)(2,1)} %all-gather.3.cloned.1.call-done) | data formatting | bytes 21299200
  196.5 443.6 %while.21 = (s32[]{:T(128)}, f32[1664,3200]{1,0:T(8,128)}, bf16[5,32,1664]{2,1,0:T(8,128)(2,1)S(1)}, bf16[32,3200]{1,0:T(8,128)(2,1)S(1)}, bf16[32,1664]{1,0:T(8...) while((s32[]{:T(128)}, f32[1664,3200]{1,0:T(8,128)}, ...), condition=%wide.region_13.14_spmd, body=%wide.region_0.13_spmd.sunk | while | flops 690257984 | bytes 59273832 | solution.py:135
  203.5 32.2 %all-reduce.4.cloned.1.call-done = bf16[32,1664]{1,0:T(8,128)(2,1)} async-done(((bf16[32,1664]{1,0:T(8,128)(2,1)}), bf16[32,1664]{1,0:T(8,128)(2,1)}) %all-reduce.4.cloned.1.call-update) | async-done | bytes 106512 | tf_op jit(solution)/shard_map/while/body/eval_jaxpr/psum | solution.py:118
  251.8 47.5 %all-reduce.4.cloned.1.call-done = bf16[32,1664]{1,0:T(8,128)(2,1)} async-done(((bf16[32,1664]{1,0:T(8,128)(2,1)}), bf16[32,1664]{1,0:T(8,128)(2,1)}) %all-reduce.4.cloned.1.call-update) | async-done | bytes 106512 | tf_op jit(solution)/shard_map/while/body/eval_jaxpr/psum | solution.py:118
  315.4 49.2 %all-reduce.4.cloned.1.call-done = bf16[32,1664]{1,0:T(8,128)(2,1)} async-done(((bf16[32,1664]{1,0:T(8,128)(2,1)}), bf16[32,1664]{1,0:T(8,128)(2,1)}) %all-reduce.4.cloned.1.call-update) | async-done | bytes 106512 | tf_op jit(solution)/shard_map/while/body/eval_jaxpr/psum | solution.py:118
  377.1 9.3 %conditional.4 = (bf16[32,1664]{1,0:T(8,128)(2,1)S(1)}, bf16[32,3200]{1,0:T(8,128)(2,1)S(1)}, bf16[32,1664]{1,0:T(8,128)(2,1)}, bf16[32,3200]{1,0:T(8,128)(2,1)}) conditional(s32[]{:T(128)} %clamp.6, () %tuple.65, (bf16[32,1664]{1,0:T(8,128)(2,1)S(1)}, f32[1,1664]{1,0:T(1,128)S(1)}, bf16[1664,3200]{1,0:T(8,128)(2,1)}, ...), branch_computations={%region_1.1_spmd, %region_2.2_spmd, %region_3.5_spmd} | conditional | flops 342601760 | bytes 12227238 | solution.py:110
  388.7 41.3 %all-reduce.4.cloned.1.call-done = bf16[32,1664]{1,0:T(8,128)(2,1)} async-done(((bf16[32,1664]{1,0:T(8,128)(2,1)}), bf16[32,1664]{1,0:T(8,128)(2,1)}) %all-reduce.4.cloned.1.call-update) | async-done | bytes 106512 | tf_op jit(solution)/shard_map/while/body/eval_jaxpr/psum | solution.py:118
  433.5 17.3 %conditional.5 = (f32[1664,3200]{1,0:T(8,128)}) conditional(s32[]{:T(128)} %convert_element_type.179, f32[1664,3200]{1,0:T(8,128)} %get-tuple-element.404, (bf16[32,1664]{1,0:T(8,128)(2,1)}, bf16[32,3200]{1,0:T(8,128)(2,1)}, f32[1664,3200]{1,0:T(8,128)}) %tuple.68), branch_computations={%region_6.6_spmd, %region_7.7_spmd} | conditional | flops 346112000 | bytes 42909704 | solution.py:124
  433.5 17.3 %convolution_add_fusion = f32[1664,3200]{1,0:T(8,128)} fusion(f32[1664,3200]{1,0:T(8,128)} %get-tuple-element.188, bf16[32,1664]{1,0:T(8,128)(2,1)} %get-tuple-element.189, bf16[32,3200]{1,0:T(8,128)(2,1)} %get-tuple-element.190), kind=kOutput, calls=%fused_computation | convolution fusion | flops 346112000 | bytes 42909696 | tf_op jit(solution)/shard_map/while/body/eval_jaxpr/cond/branch_1_fun/dot_general | solution.py:52
  465.7 29.7 %all-reduce.4.cloned.1.call-done = bf16[32,1664]{1,0:T(8,128)(2,1)} async-done(((bf16[32,1664]{1,0:T(8,128)(2,1)}), bf16[32,1664]{1,0:T(8,128)(2,1)}) %all-reduce.4.cloned.1.call-update) | async-done | bytes 106512 | tf_op jit(solution)/shard_map/while/body/eval_jaxpr/psum | solution.py:118
  498.9 17.3 %conditional.5 = (f32[1664,3200]{1,0:T(8,128)}) conditional(s32[]{:T(128)} %convert_element_type.179, f32[1664,3200]{1,0:T(8,128)} %get-tuple-element.404, (bf16[32,1664]{1,0:T(8,128)(2,1)}, bf16[32,3200]{1,0:T(8,128)(2,1)}, f32[1664,3200]{1,0:T(8,128)}) %tuple.68), branch_computations={%region_6.6_spmd, %region_7.7_spmd} | conditional | flops 346112000 | bytes 42909704 | solution.py:124
  498.9 17.3 %convolution_add_fusion = f32[1664,3200]{1,0:T(8,128)} fusion(f32[1664,3200]{1,0:T(8,128)} %get-tuple-element.188, bf16[32,1664]{1,0:T(8,128)(2,1)} %get-tuple-element.189, bf16[32,3200]{1,0:T(8,128)(2,1)} %get-tuple-element.190), kind=kOutput, calls=%fused_computation | convolution fusion | flops 346112000 | bytes 42909696 | tf_op jit(solution)/shard_map/while/body/eval_jaxpr/cond/branch_1_fun/dot_general | solution.py:52
  531.1 26.4 %all-reduce.4.cloned.1.call-done = bf16[32,1664]{1,0:T(8,128)(2,1)} async-done(((bf16[32,1664]{1,0:T(8,128)(2,1)}), bf16[32,1664]{1,0:T(8,128)(2,1)}) %all-reduce.4.cloned.1.call-update) | async-done | bytes 106512 | tf_op jit(solution)/shard_map/while/body/eval_jaxpr/psum | solution.py:118
  561.0 17.3 %conditional.5 = (f32[1664,3200]{1,0:T(8,128)}) conditional(s32[]{:T(128)} %convert_element_type.179, f32[1664,3200]{1,0:T(8,128)} %get-tuple-element.404, (bf16[32,1664]{1,0:T(8,128)(2,1)}, bf16[32,3200]{1,0:T(8,128)(2,1)}, f32[1664,3200]{1,0:T(8,128)}) %tuple.68), branch_computations={%region_6.6_spmd, %region_7.7_spmd} | conditional | flops 346112000 | bytes 42909704 | solution.py:124
  561.0 17.3 %convolution_add_fusion = f32[1664,3200]{1,0:T(8,128)} fusion(f32[1664,3200]{1,0:T(8,128)} %get-tuple-element.188, bf16[32,1664]{1,0:T(8,128)(2,1)} %get-tuple-element.189, bf16[32,3200]{1,0:T(8,128)(2,1)} %get-tuple-element.190), kind=kOutput, calls=%fused_computation | convolution fusion | flops 346112000 | bytes 42909696 | tf_op jit(solution)/shard_map/while/body/eval_jaxpr/cond/branch_1_fun/dot_general | solution.py:52
  593.1 26.1 %all-reduce.4.cloned.1.call-done = bf16[32,1664]{1,0:T(8,128)(2,1)} async-done(((bf16[32,1664]{1,0:T(8,128)(2,1)}), bf16[32,1664]{1,0:T(8,128)(2,1)}) %all-reduce.4.cloned.1.call-update) | async-done | bytes 106512 | tf_op jit(solution)/shard_map/while/body/eval_jaxpr/psum | solution.py:118
  622.7 17.3 %conditional.5 = (f32[1664,3200]{1,0:T(8,128)}) conditional(s32[]{:T(128)} %convert_element_type.179, f32[1664,3200]{1,0:T(8,128)} %get-tuple-element.404, (bf16[32,1664]{1,0:T(8,128)(2,1)}, bf16[32,3200]{1,0:T(8,128)(2,1)}, f32[1664,3200]{1,0:T(8,128)}) %tuple.68), branch_computations={%region_6.6_spmd, %region_7.7_spmd} | conditional | flops 346112000 | bytes 42909704 | solution.py:124
  622.8 17.3 %convolution_add_fusion = f32[1664,3200]{1,0:T(8,128)} fusion(f32[1664,3200]{1,0:T(8,128)} %get-tuple-element.188, bf16[32,1664]{1,0:T(8,128)(2,1)} %get-tuple-element.189, bf16[32,3200]{1,0:T(8,128)(2,1)} %get-tuple-element.190), kind=kOutput, calls=%fused_computation | convolution fusion | flops 346112000 | bytes 42909696 | tf_op jit(solution)/shard_map/while/body/eval_jaxpr/cond/branch_1_fun/dot_general | solution.py:52
  640.1 12.3 %convert_element_type.68 = bf16[1664,3200]{1,0:T(8,128)(2,1)} convert(f32[1664,3200]{1,0:T(8,128)} %get-tuple-element.215) | non-fusion elementwise | flops 5324800 | bytes 31948800 | tf_op jit(solution)/shard_map/convert_element_type | solution.py:138
  652.4 150.3 %fusion = bf16[64,3200]{1,0:T(8,128)(2,1)S(1)} fusion(bf16[1664,3200]{1,0:T(8,128)(2,1)} %convert_element_type.68), kind=kCustom, calls=%all-reduce-scatter | all-reduce-scatter fusion | flops 6553601 | bytes 11060224
  817.5 11.5 %collective-permute-done.7 = bf16[52,3200]{1,0:T(8,128)(2,1)S(1)} collective-permute-done((bf16[52,3200]{1,0:T(8,128)(2,1)S(1)}, bf16[52,3200]{1,0:T(8,128)(2,1)S(1)}, u32[]{:S(2)}, u32[]{:S(2)}) %collective-permute-start.7) | collective-permute-done | bytes 332832
  842.7 46.2 %collective-permute-done.6 = bf16[64,3200]{1,0:T(8,128)(2,1)} collective-permute-done((bf16[64,3200]{1,0:T(8,128)(2,1)S(1)}, bf16[64,3200]{1,0:T(8,128)(2,1)}, u32[]{:S(2)}, u32[]{:S(2)}) %collective-permute-start.6) | collective-permute-done | bytes 409632
  888.8 21.1 %concatenate = bf16[436,3200]{1,0:T(8,128)(2,1)S(1)} concatenate(bf16[52,3200]{1,0:T(8,128)(2,1)} %copy-done.6, bf16[64,3200]{1,0:T(8,128)(2,1)} %collective-permute-done.6, bf16[64,3200]{1,0:T(8,128)(2,1)} %copy-done.5, bf16[64,3200]{1,0:T(8,128)(2,1)} %copy-done.4, bf16[64,3200]{1,0:T(8,128)(2,1)} %copy-done.3, bf16[64,3200]{1,0:T(8,128)(2,1)} %copy-done.2, ...), dimensions={0} | concatenate | bytes 5580800
  (228 shorter events, 190.2 us)
Async XLA Ops:
  7.2 165.5 %all-gather.3.cloned.1.call-start = ((), (), s32[]{:S(2)}) async-start(), calls=%async_computation | async-start | bytes 21964800 | tf_op jit(solution)/shard_map/all_gather | solution.py:70
  196.5 39.1 %all-reduce.4.cloned.1.call-start = ((), (), s32[]{:S(2)}) async-start(), calls=%async_computation.1 | async-start | bytes 212992 | tf_op jit(solution)/shard_map/while/body/eval_jaxpr/psum | solution.py:118
  201.9 37.2 %collective-permute-start = (bf16[32,3200]{1,0:T(8,128)(2,1)S(1)}, bf16[32,3200]{1,0:T(8,128)(2,1)S(1)}, u32[]{:S(2)}, u32[]{:S(2)}) collective-permute-start(bf16[32,3200]{1,0:T(8,128)(2,1)S(1)} %get-tuple-element.368), channel_id=1, source_target_pairs={{64,0},{128,64},{192,128},{65,1},{129,65},{193,129},{66,2},{130,66... | collective-permute-start | bytes 614408 | tf_op jit(solution)/shard_map/while/body/eval_jaxpr/ppermute | solution.py:22
  244.9 54.4 %all-reduce.4.cloned.1.call-start = ((), (), s32[]{:S(2)}) async-start(), calls=%async_computation.1 | async-start | bytes 212992 | tf_op jit(solution)/shard_map/while/body/eval_jaxpr/psum | solution.py:118
  250.2 52.5 %collective-permute-start = (bf16[32,3200]{1,0:T(8,128)(2,1)S(1)}, bf16[32,3200]{1,0:T(8,128)(2,1)S(1)}, u32[]{:S(2)}, u32[]{:S(2)}) collective-permute-start(bf16[32,3200]{1,0:T(8,128)(2,1)S(1)} %get-tuple-element.368), channel_id=1, source_target_pairs={{64,0},{128,64},{192,128},{65,1},{129,65},{193,129},{66,2},{130,66... | collective-permute-start | bytes 614408 | tf_op jit(solution)/shard_map/while/body/eval_jaxpr/ppermute | solution.py:22
  308.5 56.1 %all-reduce.4.cloned.1.call-start = ((), (), s32[]{:S(2)}) async-start(), calls=%async_computation.1 | async-start | bytes 212992 | tf_op jit(solution)/shard_map/while/body/eval_jaxpr/psum | solution.py:118
  313.9 54.3 %collective-permute-start = (bf16[32,3200]{1,0:T(8,128)(2,1)S(1)}, bf16[32,3200]{1,0:T(8,128)(2,1)S(1)}, u32[]{:S(2)}, u32[]{:S(2)}) collective-permute-start(bf16[32,3200]{1,0:T(8,128)(2,1)S(1)} %get-tuple-element.368), channel_id=1, source_target_pairs={{64,0},{128,64},{192,128},{65,1},{129,65},{193,129},{66,2},{130,66... | collective-permute-start | bytes 614408 | tf_op jit(solution)/shard_map/while/body/eval_jaxpr/ppermute | solution.py:22
  373.9 56.1 %all-reduce.4.cloned.1.call-start = ((), (), s32[]{:S(2)}) async-start(), calls=%async_computation.1 | async-start | bytes 212992 | tf_op jit(solution)/shard_map/while/body/eval_jaxpr/psum | solution.py:118
  387.2 63.6 %collective-permute-start = (bf16[32,3200]{1,0:T(8,128)(2,1)S(1)}, bf16[32,3200]{1,0:T(8,128)(2,1)S(1)}, u32[]{:S(2)}, u32[]{:S(2)}) collective-permute-start(bf16[32,3200]{1,0:T(8,128)(2,1)S(1)} %get-tuple-element.368), channel_id=1, source_target_pairs={{64,0},{128,64},{192,128},{65,1},{129,65},{193,129},{66,2},{130,66... | collective-permute-start | bytes 614408 | tf_op jit(solution)/shard_map/while/body/eval_jaxpr/ppermute | solution.py:22
  432.2 18.6 %collective-permute-start.1 = (bf16[32,1664]{1,0:T(8,128)(2,1)S(1)}, bf16[32,1664]{1,0:T(8,128)(2,1)S(1)}, u32[]{:S(2)}, u32[]{:S(2)}) collective-permute-start(bf16[32,1664]{1,0:T(8,128)(2,1)S(1)} %get-tuple-element.369), channel_id=1, source_target_pairs={{64,0},{128,64},{192,128},{65,1},{129,65},{193,129},{66,2},{130,66... | collective-permute-start | bytes 319496 | tf_op jit(solution)/shard_map/while/body/eval_jaxpr/ppermute | solution.py:22
  450.8 44.6 %all-reduce.4.cloned.1.call-start = ((), (), s32[]{:S(2)}) async-start(), calls=%async_computation.1 | async-start | bytes 212992 | tf_op jit(solution)/shard_map/while/body/eval_jaxpr/psum | solution.py:118
  464.1 52.1 %collective-permute-start = (bf16[32,3200]{1,0:T(8,128)(2,1)S(1)}, bf16[32,3200]{1,0:T(8,128)(2,1)S(1)}, u32[]{:S(2)}, u32[]{:S(2)}) collective-permute-start(bf16[32,3200]{1,0:T(8,128)(2,1)S(1)} %get-tuple-element.368), channel_id=1, source_target_pairs={{64,0},{128,64},{192,128},{65,1},{129,65},{193,129},{66,2},{130,66... | collective-permute-start | bytes 614408 | tf_op jit(solution)/shard_map/while/body/eval_jaxpr/ppermute | solution.py:22
  497.6 18.6 %collective-permute-start.1 = (bf16[32,1664]{1,0:T(8,128)(2,1)S(1)}, bf16[32,1664]{1,0:T(8,128)(2,1)S(1)}, u32[]{:S(2)}, u32[]{:S(2)}) collective-permute-start(bf16[32,1664]{1,0:T(8,128)(2,1)S(1)} %get-tuple-element.369), channel_id=1, source_target_pairs={{64,0},{128,64},{192,128},{65,1},{129,65},{193,129},{66,2},{130,66... | collective-permute-start | bytes 319496 | tf_op jit(solution)/shard_map/while/body/eval_jaxpr/ppermute | solution.py:22
  516.2 41.3 %all-reduce.4.cloned.1.call-start = ((), (), s32[]{:S(2)}) async-start(), calls=%async_computation.1 | async-start | bytes 212992 | tf_op jit(solution)/shard_map/while/body/eval_jaxpr/psum | solution.py:118
  529.5 48.7 %collective-permute-start = (bf16[32,3200]{1,0:T(8,128)(2,1)S(1)}, bf16[32,3200]{1,0:T(8,128)(2,1)S(1)}, u32[]{:S(2)}, u32[]{:S(2)}) collective-permute-start(bf16[32,3200]{1,0:T(8,128)(2,1)S(1)} %get-tuple-element.368), channel_id=1, source_target_pairs={{64,0},{128,64},{192,128},{65,1},{129,65},{193,129},{66,2},{130,66... | collective-permute-start | bytes 614408 | tf_op jit(solution)/shard_map/while/body/eval_jaxpr/ppermute | solution.py:22
  578.3 41.0 %all-reduce.4.cloned.1.call-start = ((), (), s32[]{:S(2)}) async-start(), calls=%async_computation.1 | async-start | bytes 212992 | tf_op jit(solution)/shard_map/while/body/eval_jaxpr/psum | solution.py:118
  591.6 48.5 %collective-permute-start = (bf16[32,3200]{1,0:T(8,128)(2,1)S(1)}, bf16[32,3200]{1,0:T(8,128)(2,1)S(1)}, u32[]{:S(2)}, u32[]{:S(2)}) collective-permute-start(bf16[32,3200]{1,0:T(8,128)(2,1)S(1)} %get-tuple-element.368), channel_id=1, source_target_pairs={{64,0},{128,64},{192,128},{65,1},{129,65},{193,129},{66,2},{130,66... | collective-permute-start | bytes 614408 | tf_op jit(solution)/shard_map/while/body/eval_jaxpr/ppermute | solution.py:22
  621.4 18.6 %collective-permute-start.1 = (bf16[32,1664]{1,0:T(8,128)(2,1)S(1)}, bf16[32,1664]{1,0:T(8,128)(2,1)S(1)}, u32[]{:S(2)}, u32[]{:S(2)}) collective-permute-start(bf16[32,1664]{1,0:T(8,128)(2,1)S(1)} %get-tuple-element.369), channel_id=1, source_target_pairs={{64,0},{128,64},{192,128},{65,1},{129,65},{193,129},{66,2},{130,66... | collective-permute-start | bytes 319496 | tf_op jit(solution)/shard_map/while/body/eval_jaxpr/ppermute | solution.py:22
  802.8 26.2 %collective-permute-start.7 = (bf16[52,3200]{1,0:T(8,128)(2,1)S(1)}, bf16[52,3200]{1,0:T(8,128)(2,1)S(1)}, u32[]{:S(2)}, u32[]{:S(2)}) collective-permute-start(bf16[52,3200]{1,0:T(8,128)(2,1)S(1)} %slice.4), channel_id=1, source_target_pairs={{0,12},{2,14},{4,16},{6,18},{8,20},{10,22},{12,24},{14,26},{16,28}... | collective-permute-start | bytes 998408
  806.0 33.6 %collective-permute-start.2 = (bf16[64,3200]{1,0:T(8,128)(2,1)S(1)}, bf16[64,3200]{1,0:T(8,128)(2,1)S(1)}, u32[]{:S(2)}, u32[]{:S(2)}) collective-permute-start(bf16[64,3200]{1,0:T(8,128)(2,1)S(1)} %fusion), channel_id=1, source_target_pairs={{0,2},{2,4},{4,6},{6,8},{8,10},{10,12},{12,14},{14,16},{16,18},{18... | collective-permute-start | bytes 1228808
  807.9 33.1 %collective-permute-start.3 = (bf16[64,3200]{1,0:T(8,128)(2,1)S(1)}, bf16[64,3200]{1,0:T(8,128)(2,1)S(1)}, u32[]{:S(2)}, u32[]{:S(2)}) collective-permute-start(bf16[64,3200]{1,0:T(8,128)(2,1)S(1)} %fusion), channel_id=1, source_target_pairs={{0,4},{2,6},{4,8},{6,10},{8,12},{10,14},{12,16},{14,18},{16,20},{1... | collective-permute-start | bytes 1228808
  813.7 27.3 %collective-permute-start.4 = (bf16[64,3200]{1,0:T(8,128)(2,1)S(1)}, bf16[64,3200]{1,0:T(8,128)(2,1)S(1)}, u32[]{:S(2)}, u32[]{:S(2)}) collective-permute-start(bf16[64,3200]{1,0:T(8,128)(2,1)S(1)} %fusion), channel_id=1, source_target_pairs={{0,6},{2,8},{4,10},{6,12},{8,14},{10,16},{12,18},{14,20},{16,22},{... | collective-permute-start | bytes 1228808
  815.6 25.4 %collective-permute-start.5 = (bf16[64,3200]{1,0:T(8,128)(2,1)S(1)}, bf16[64,3200]{1,0:T(8,128)(2,1)S(1)}, u32[]{:S(2)}, u32[]{:S(2)}) collective-permute-start(bf16[64,3200]{1,0:T(8,128)(2,1)S(1)} %fusion), channel_id=1, source_target_pairs={{0,8},{2,10},{4,12},{6,14},{8,16},{10,18},{12,20},{14,22},{16,24},... | collective-permute-start | bytes 1228808
  829.0 59.8 %collective-permute-start.6 = (bf16[64,3200]{1,0:T(8,128)(2,1)S(1)}, bf16[64,3200]{1,0:T(8,128)(2,1)}, u32[]{:S(2)}, u32[]{:S(2)}) collective-permute-start(bf16[64,3200]{1,0:T(8,128)(2,1)S(1)} %fusion), channel_id=1, source_target_pairs={{0,10},{2,12},{4,14},{6,16},{8,18},{10,20},{12,22},{14,24},{16,26}... | collective-permute-start | bytes 1228808
  (18 other events, 233.4 us)
Sparse Core Ops, SparseCore 0:
  10.6 161.9 all-gather.2
  202.0 33.5 all-reduce.3
  250.4 48.8 all-reduce.3
  314.0 50.5 all-reduce.3
  387.3 42.6 all-reduce.3
  464.3 31.0 all-reduce.3
  529.6 27.7 all-reduce.3
  591.7 27.4 all-reduce.3
where the time goes:
time: 920 us; the launch traced here: 918 us
  waiting for transfers between devices  498 us (54%)
  blocking collectives  150 us (16%)
  matrix products  99.5 us (11%)
  local copies, waits for them, and re-layouts  70.8 us (8%)
  other arithmetic  45.2 us (5%)
  starting transfers between devices  33.6 us (4%)
  between operations  14.8 us (2%)
    psum x7, waiting for transfers between devices, advance(): lax.psum(shortened(partial_value), 'tensor')  252 us
    all_gather x1, waiting for transfers between devices, body(): full_weight = lax.all_gather(weights[0], 'dp', axis=0, tiled=True)  161 us
    unnamed x1, blocking collectives  150 us
    dot_general x4, matrix products, add_term(): lax.dot_general(left_side, right_side, (((0,), (0,)), ((), ())), preferre...  69.1 us
    unnamed x7, waiting for transfers between devices  66.9 us
    unnamed x19, local copies, waits for them, and re-layouts  41.1 us
    dot_general x4, matrix products, up_work(): lax.dot_general(act_grad, full_weight, (((1,), (1,)), ((), ())), preferre...  29 us
  transfers between devices with their start and end apart: 28, of which 15 were waited for; matrix products, arithmetic and copies ran while one was open for 10% of the time, Pallas kernels for 0%

commit v1 on v0

v1 whole, which is shorter than its diff:
```python
import functools

import jax
import jax.numpy as jnp
from jax import lax
from jax.experimental import pallas as pl
from jax.experimental.pallas import tpu as pltpu
from jax.sharding import PartitionSpec as P

norm_eps = 1e-06
root_half = 0.7071067811865476
inv_root_two_pi = 0.3989422804014327

MESH = pl.DeviceIdType.MESH
f32 = jnp.float32
bf16 = jnp.bfloat16

NX, NY, NZ = 4, 4, 8
GROUP = NX * NY
D = 1664
ROWS = 32
HALF = 16
TOK = 512
OWN = 52
PAD = 64
PACK = NX * OWN
LANE = 128
WIDE = 256
BLOCKS = 25
SECTIONS = 4


def first_block(piece):
    return (23 * piece) // 15


def gelu_value(p):
    return p * (0.5 * (1.0 + lax.erf(p * root_half)))


def gelu_slope(p):
    cdf = 0.5 * (1.0 + lax.erf(p * root_half))
    return cdf + p * (jnp.exp(-0.5 * p * p) * inv_root_two_pi)


def kernel(
    llm, slots, counts, xin, pre, w, scale,
    wout, gout,
    wx, wg, preb, full, scaled, part, sibs, sibr, rss, rsr, act, slope, agrad,
    dwp, zs, zr, outs, outr, scl, xi, g0f, g0s,
    local_sem, wx_s, wx_r, pre_s, pre_r, sc_s, sc_r, xi_s, xi_r,
    ag_s, ag_r, sib_s, sib_r, cs_s, cs_r, rs_s, rs_r,
    zag_s, zag_r, zrs_s, zrs_r, out_s, out_r, g0_s, g0_r, g1_s, g1_r,
):
    y = lax.axis_index("pipe")
    dp = lax.axis_index("dp")
    c = lax.axis_index("tensor")
    z = lax.div(dp, NX)
    x = lax.rem(dp, NX)
    gid = x * NY + y
    oc = 1 - c
    sibling = (y, dp, oc)
    up_z = (y, lax.rem(z + 1, NZ) * NX + x, c)
    down_z = (y, lax.rem(z + NZ - 1, NZ) * NX + x, c)

    def place(piece):
        return (lax.rem(piece, NY), z * NX + lax.div(piece, NY), c)

    def other(k):
        return lax.rem(gid + k, GROUP)

    def loop(low, high, body):
        def step(k, carry):
            body(k)
            return carry

        lax.fori_loop(low, high, step, 0)

    def remote(src, dst, send, recv, where):
        return pltpu.make_async_remote_copy(
            src_ref=src, dst_ref=dst, send_sem=send, recv_sem=recv, device_id=where, device_id_type=MESH
        )

    def take(ref, sem):
        pltpu.make_async_copy(ref, ref, sem).wait()

    def columns(piece):
        return pl.ds(pl.multiple_of(lax.div(23 * piece, 15) * LANE, LANE), WIDE)

    barrier = pltpu.get_barrier_semaphore()

    def greet(k):
        pl.semaphore_signal(barrier, inc=1, device_id=place(other(k)), device_id_type=MESH)

    loop(1, GROUP, greet)
    for where in (sibling, up_z, down_z):
        pl.semaphore_signal(barrier, inc=1, device_id=where, device_id_type=MESH)
    pl.semaphore_wait(barrier, GROUP + 2)

    own_w = pltpu.make_async_copy(w.at[:, columns(gid)], wx.at[y * NX + x], local_sem.at[0])
    own_w.start()
    own_pre = pltpu.make_async_copy(pre.at[:, columns(gid)], preb.at[y * NX + x], local_sem.at[1])
    own_pre.start()

    def send_w(k):
        p = other(k)
        remote(w.at[:, columns(p)], wx.at[y * NX + x], wx_s, wx_r, place(p)).start()

    loop(1, GROUP, send_w)

    scl[y] = scale[...]

    def send_scale(k):
        py = lax.rem(y + k, NY)
        remote(scale, scl.at[y], sc_s, sc_r, (py, dp, c)).start()

    loop(1, NY, send_scale)

    slot_line = slots[pl.ds(y, 1), :]
    row_ids = lax.broadcasted_iota(jnp.int32, (HALF, ROWS), 0) + c * HALF
    slot_ids = lax.broadcasted_iota(jnp.int32, (HALF, ROWS), 1)
    hit = (slot_line == row_ids) & (slot_ids < counts[0, y])
    onehot = jnp.where(hit, 1.0, 0.0).astype(bf16)
    full[0, gid, c] = jnp.dot(onehot, llm[y], preferred_element_type=f32).astype(bf16)

    def ag_send(i):
        def send(k):
            mine = full.at[i, gid, c]
            remote(mine, mine, ag_s.at[i], ag_r.at[i], place(other(k))).start()

        loop(1, GROUP, send)

    def ag_forward(i):
        take(full.at[i, pl.ds(0, GROUP - 1), 0], ag_r.at[i])
        half = full.at[i, :, c]
        remote(half, half, sib_s.at[i], sib_r.at[i], sibling).start()

    def ag_finish(i):
        take(full.at[i, :, oc], sib_r.at[i])

    ag_send(0)

    def send_pre(k):
        p = other(k)
        remote(pre.at[:, columns(p)], preb.at[y * NX + x], pre_s, pre_r, place(p)).start()

    loop(1, GROUP, send_pre)

    half_rows = pl.ds(pl.multiple_of(c * HALF, HALF), HALF)
    for b, s in ((0, 2), (1, 0)):

        @pl.when(y == s)
        def _():
            xi[b] = xin[y, half_rows, :]

            def send(k):
                py = lax.rem(y + k, NY)
                remote(xin.at[py, half_rows, :], xi.at[b], xi_s.at[b], xi_r.at[b], (py, dp, c)).start()

            loop(1, NY, send)

    take(wx.at[pl.ds(0, GROUP - 1)], wx_r)
    own_w.wait()
    to_row = lax.broadcasted_iota(jnp.int32, (PACK, NX * PAD), 0)
    from_row = lax.broadcasted_iota(jnp.int32, (PACK, NX * PAD), 1)
    from_block = lax.shift_right_logical(from_row, 6)
    inside = from_row - from_block * PAD
    picks = (inside < OWN) & (from_block * OWN + inside == to_row)
    pick = jnp.where(picks, 1.0, 0.0).astype(bf16)

    def pack(s):
        blocks = wx[s * NX : (s + 1) * NX].reshape(NX * PAD, WIDE)
        wg[s, z] = jnp.dot(pick, blocks, preferred_element_type=f32).astype(bf16)

    def zag_block(s, chunk, d, k):
        if k == 4:
            return wg.at[s, chunk, :, pl.ds(d * LANE, LANE)]
        return wg.at[s, chunk]

    def zag_take(s, k):
        for d, chunk in ((0, lax.rem(z - k + NZ, NZ)), (1, lax.rem(z + k, NZ))):
            take(zag_block(s, chunk, d, k), zag_r.at[s, d, k - 1])

    def zag(s, k):
        if k > 1:
            zag_take(s, k - 1)
        for d, chunk, where in (
            (0, lax.rem(z - k + 1 + NZ, NZ), up_z),
            (1, lax.rem(z + k - 1, NZ), down_z),
        ):
            block = zag_block(s, chunk, d, k)
            remote(block, block, zag_s.at[s, d, k - 1], zag_r.at[s, d, k - 1], where).start()

    def zrs(s, k):
        ways = ((0, lax.rem(z + 5 - k + NZ, NZ), up_z), (1, lax.rem(z - 5 + k + NZ, NZ), down_z))
        for d, chunk, where in ways:
            rows = pl.ds(pl.multiple_of(chunk * PACK, HALF), PACK)
            side = pl.ds(d * LANE, LANE)
            if k == 1:
                zs[s, d, 0, :, side] = dwp[s, rows, side].astype(bf16)
                src, dst = zs.at[s, d, 0, :, side], zr.at[s, d, 0, :, side]
            else:
                if k == 2:
                    take(zr.at[s, d, 0, :, side], zrs_r.at[s, d, 0])
                    there = pl.ds((1 - d) * LANE, LANE)
                    zs[s, d, 1, :, side] = (dwp[s, rows, side] + zr[s, d, 0, :, side].astype(f32)).astype(bf16)
                    zs[s, d, 1, :, there] = dwp[s, rows, there].astype(bf16)
                else:
                    take(zr.at[s, d, k - 2], zrs_r.at[s, d, k - 2])
                    zs[s, d, k - 1] = (dwp[s, rows, :] + zr[s, d, k - 2].astype(f32)).astype(bf16)
                src, dst = zs.at[s, d, k - 1], zr.at[s, d, k - 1]
            remote(src, dst, zrs_s.at[s, d, k - 1], zrs_r.at[s, d, k - 1], where).start()

    def zrs_finish(s):
        for d in range(2):
            take(zr.at[s, d, 3], zrs_r.at[s, d, 3])
        rows = pl.ds(pl.multiple_of(z * PACK, HALF), PACK)
        total = dwp[s, rows, :] + zr[s, 0, 3].astype(f32) + zr[s, 1, 3].astype(f32)
        spread = lax.dot_general(pick, total.astype(bf16), (((0,), (0,)), ((), ())), preferred_element_type=f32)
        outs[s * NX : (s + 1) * NX] = spread.astype(bf16).reshape(NX, PAD, WIDE)

        def send(px):
            mine = (y == s) & (px == x)

            @pl.when(mine)
            def _():
                outr[gid] = outs[s * NX + px]

            @pl.when(jnp.logical_not(mine))
            def _():
                remote(outs.at[s * NX + px], outr.at[gid], out_s, out_r, (s, z * NX + px, c)).start()

        loop(0, NX, send)

    pack(3)
    zag(3, 1)
    pack(2)
    zag(2, 1)
    pack(1)
    pack(0)

    take(scl.at[pl.ds(0, NY - 1)], sc_r)

    def unit_rows(b):
        values = xi[b].astype(f32)
        center = values - jnp.mean(values, axis=-1, keepdims=True)
        inv_std = lax.rsqrt(jnp.mean(center * center, axis=-1, keepdims=True) + norm_eps)
        return center * inv_std, inv_std

    for b, s in ((0, 2), (1, 0)):

        @pl.when(y != s)
        def _():
            take(xi.at[b], xi_r.at[b])

        unit, inv_std = unit_rows(b)
        full[1 + 2 * b, gid, c] = (unit * scl[s]).astype(bf16)

    ag_send(1)
    zag(3, 2)
    zag(2, 2)
    ag_forward(0)
    zag(3, 3)
    zag(2, 3)

    def scale_rows(i, s):
        def one(p):
            rows = full[2 * i, p].astype(f32) * scl[s]
            scaled[i, p] = rows.astype(bf16)

        loop(0, GROUP, one)

    ag_finish(0)
    scale_rows(0, 3)
    zag(3, 4)
    zag(2, 4)

    def gelu_rows(b, down, up):
        def one(p):
            rows = pl.ds(pl.multiple_of(lax.rem(p, NY) * ROWS, ROWS), ROWS)
            at = pl.ds(pl.multiple_of(p * ROWS, ROWS), ROWS)
            act[b, at, :] = gelu_value(preb[down * NX + lax.div(p, NY), rows, :].astype(f32)).astype(bf16)
            slope[b, at, :] = gelu_slope(preb[up * NX + lax.div(p, NY), rows, :].astype(f32))

        loop(0, GROUP, one)

    take(preb.at[pl.ds(0, GROUP - 1)], pre_r)
    own_pre.wait()
    gelu_rows(0, 3, 2)

    repeated = jnp.where((lax.rem(gid, 2) == 1) & (gid < 14), LANE, 0)
    keep = lax.broadcasted_iota(jnp.int32, (WIDE, WIDE), 1) >= repeated

    def hidden_back(b, down):
        weight = wg[down].reshape(D, WIDE)
        for t in range(2):
            left = scaled[b, t * 8 : t * 8 + 8].reshape(WIDE, D)
            hidden = jnp.dot(left, weight, preferred_element_type=f32).astype(bf16).astype(f32)
            at = pl.ds(t * WIDE, WIDE)
            agrad[b, at, :] = (hidden * slope[b, at, :]).astype(bf16)

    def norm_part(b, up):
        weight = wg[up].reshape(D, WIDE)
        for t in range(2):
            rows = agrad[b, pl.ds(t * WIDE, WIDE), :]
            rows = jnp.where(keep, rows, jnp.zeros_like(rows))
            product = lax.dot_general(rows, weight, (((1,), (1,)), ((), ())), preferred_element_type=f32)
            part[t * 8 : t * 8 + 8] = product.reshape(8, 2, HALF, D)

    def rs_start(b):
        def one(p):
            sibs[b, p] = part[p, oc].astype(bf16)

        loop(0, GROUP, one)
        remote(sibs.at[b], sibr.at[b], cs_s.at[b], cs_r.at[b], sibling).start()

    def rs_middle(b):
        take(sibr.at[b], cs_r.at[b])

        def one(k):
            p = other(k)
            rss[b, p] = (part[p, c] + sibr[b, p].astype(f32)).astype(bf16)
            remote(rss.at[b, p], rsr.at[b, gid], rs_s.at[b], rs_r.at[b], place(p)).start()

        loop(1, GROUP, one)

    def rs_finish(b, s):
        take(rsr.at[b, pl.ds(0, GROUP - 1)], rs_r.at[b])
        total = part[gid, c] + sibr[b, gid].astype(f32)

        def add(k, so_far):
            return so_far + rsr[b, other(k)].astype(f32)

        total = lax.fori_loop(1, GROUP, add, total)
        unit, inv_std = unit_rows(b)
        back = total * scl[s]
        back = inv_std * (
            back
            - jnp.mean(back, axis=-1, keepdims=True)
            - unit * jnp.mean(back * unit, axis=-1, keepdims=True)
        )
        return (full[2 * b, gid, c].astype(f32) + back).astype(bf16)

    def weight_part(s, left_ref, right):
        for low, size in ((0, 512), (512, 512), (1024, 640)):
            left = left_ref[:, :, :, low : low + size].reshape(TOK, size)
            dwp[s, low : low + size, :] = lax.dot_general(
                left, right, (((0,), (0,)), ((), ())), preferred_element_type=f32
            )

    zag_take(3, 4)
    hidden_back(0, 3)
    zag(1, 1)
    zag(0, 1)
    zag_take(2, 4)
    norm_part(0, 2)
    rs_start(0)
    zag(1, 2)
    zag(0, 2)
    weight_part(3, scaled.at[0], act[0])
    rs_middle(0)
    zrs(3, 1)
    ag_forward(1)
    zag(1, 3)
    zag(0, 3)
    gelu_rows(1, 1, 0)
    full[2, gid, c] = rs_finish(0, 2)
    ag_send(2)
    zag(1, 4)
    zag(0, 4)
    ag_finish(1)
    weight_part(2, full.at[1], agrad[0])
    zrs(2, 1)
    zrs(3, 2)
    ag_send(3)
    ag_forward(2)
    zrs(3, 3)
    zrs(2, 2)
    ag_finish(2)
    scale_rows(1, 1)
    zag_take(1, 4)
    hidden_back(1, 1)
    zag_take(0, 4)
    norm_part(1, 0)
    rs_start(1)
    weight_part(1, scaled.at[1], act[1])
    zrs(1, 1)
    zrs(3, 4)
    zrs(2, 3)
    rs_middle(1)
    ag_forward(3)
    ag_finish(3)
    weight_part(0, full.at[3], agrad[1])
    zrs(0, 1)
    zrs(2, 4)
    zrs(1, 2)
    zrs(0, 2)
    zrs_finish(3)
    zrs(1, 3)
    zrs(0, 3)
    last = rs_finish(1, 0)

    @pl.when(y == 0)
    def _():
        g0f[0, c] = last

    @pl.when(y != 0)
    def _():
        g0s[...] = last
        remote(g0s, g0f.at[y, c], g0_s, g0_r, (0, dp, c)).start()

    zrs_finish(2)
    zrs(1, 4)
    zrs(0, 4)
    zrs_finish(1)
    zrs_finish(0)

    @pl.when(y == 0)
    def _():
        take(g0f.at[pl.ds(1, NY - 1), 0], g0_r)
        half = g0f.at[:, c]
        remote(half, half, g1_s, g1_r, sibling).start()
        take(g0f.at[:, oc], g1_r)
        gout[...] = g0f[...].reshape(NY * ROWS, D)
        take(half, g1_s)

    own = pl.ds(x * NY, NY)

    @pl.when((y == 1) | (y == 2))
    def _():
        gout[...] = full[2, own].reshape(NY * ROWS, D)

    @pl.when(y == 3)
    def _():
        gout[...] = full[0, own].reshape(NY * ROWS, D)

    take(outr.at[pl.ds(0, GROUP - 1)], out_r)
    for p in range(GROUP):
        low = first_block(p) * LANE
        wout[:, low : low + WIDE] = outr[p]

    take(wx.at[pl.ds(0, GROUP - 1)], wx_s)
    take(preb.at[pl.ds(0, GROUP - 1)], pre_s)
    take(scl.at[pl.ds(0, NY - 1)], sc_s)
    for b, s in ((0, 2), (1, 0)):

        @pl.when(y == s)
        def _():
            take(full.at[0, pl.ds(0, NY - 1), 0], xi_s.at[b])

    for i in range(4):
        take(full.at[i, pl.ds(0, GROUP - 1), 0], ag_s.at[i])
        take(full.at[i, :, c], sib_s.at[i])
    for b in range(2):
        take(sibs.at[b], cs_s.at[b])
        take(rss.at[b, pl.ds(0, GROUP - 1)], rs_s.at[b])
    for s in range(SECTIONS):
        for d in range(2):
            for k in range(1, 5):
                take(zag_block(s, 0, d, k), zag_s.at[s, d, k - 1])
                if k == 1:
                    take(zs.at[s, d, 0, :, pl.ds(d * LANE, LANE)], zrs_s.at[s, d, 0])
                else:
                    take(zs.at[s, d, k - 1], zrs_s.at[s, d, k - 1])
    take(outs.at[pl.ds(0, GROUP - 1)], out_s)

    @pl.when(y != 0)
    def _():
        take(g0s, g0_s)


def body(llm_grad, slot_row, counts, saved_in, saved_pre, weights, channel_scale):
    hidden = saved_pre.shape[3]
    padded = jnp.pad(weights[0], ((0, PAD - OWN), (0, 0)))
    pre = saved_pre.reshape(NY * ROWS, hidden)
    vmem = pl.BlockSpec(memory_space=pltpu.VMEM)
    anywhere = pl.BlockSpec(memory_space=pl.ANY)
    dma = pltpu.SemaphoreType.DMA
    scratch = [
        pltpu.VMEM((GROUP, PAD, WIDE), bf16),
        pltpu.VMEM((SECTIONS, NZ, PACK, WIDE), bf16),
        pltpu.VMEM((GROUP, NY * ROWS, WIDE), bf16),
        pltpu.VMEM((4, GROUP, 2, HALF, D), bf16),
        pltpu.VMEM((2, GROUP, 2, HALF, D), bf16),
        pltpu.VMEM((GROUP, 2, HALF, D), f32),
        pltpu.VMEM((2, GROUP, HALF, D), bf16),
        pltpu.VMEM((2, GROUP, HALF, D), bf16),
        pltpu.VMEM((2, GROUP, HALF, D), bf16),
        pltpu.VMEM((2, GROUP, HALF, D), bf16),
        pltpu.VMEM((2, TOK, WIDE), bf16),
        pltpu.VMEM((2, TOK, WIDE), f32),
        pltpu.VMEM((2, TOK, WIDE), bf16),
        pltpu.VMEM((SECTIONS, D, WIDE), f32),
        pltpu.VMEM((SECTIONS, 2, 4, PACK, WIDE), bf16),
        pltpu.VMEM((SECTIONS, 2, 4, PACK, WIDE), bf16),
        pltpu.VMEM((GROUP, PAD, WIDE), bf16),
        pltpu.VMEM((GROUP, PAD, WIDE), bf16),
        pltpu.VMEM((SECTIONS, 1, D), f32),
        pltpu.VMEM((2, HALF, D), bf16),
        pltpu.VMEM((NY, 2, HALF, D), bf16),
        pltpu.VMEM((HALF, D), bf16),
        dma((2,)), dma, dma, dma, dma, dma, dma, dma((2,)), dma((2,)),
        dma((4,)), dma((4,)), dma((4,)), dma((4,)), dma((2,)), dma((2,)), dma((2,)), dma((2,)),
        dma((4, 2, 4)), dma((4, 2, 4)), dma((4, 2, 4)), dma((4, 2, 4)), dma, dma, dma, dma, dma, dma,
    ]
    wout, gout = pl.pallas_call(
        kernel,
        out_shape=(
            jax.ShapeDtypeStruct((PAD, hidden), bf16),
            jax.ShapeDtypeStruct((NY * ROWS, D), bf16),
        ),
        in_specs=[vmem, vmem, pl.BlockSpec(memory_space=pltpu.SMEM), vmem, anywhere, anywhere, vmem],
        out_specs=(vmem, vmem),
        scratch_shapes=scratch,
        compiler_params=pltpu.CompilerParams(
            collective_id=0, has_side_effects=True, vmem_limit_bytes=60 * 1024 * 1024
        ),
    )(llm_grad, slot_row[:, 0], counts, saved_in[0], pre, padded, channel_scale)
    return (wout[None, :OWN], gout.reshape(1, NY, ROWS, D))


def solution(mesh):
    in_specs = (
        P(None, "dp", None),
        P(None, "dp", None),
        P("dp", None),
        P("pipe", None, "dp", None),
        P("pipe", None, "dp", "tensor"),
        P("pipe", "dp", "tensor"),
        P("pipe", None),
    )
    out_specs = (P("pipe", "dp", "tensor"), P("pipe", None, "dp", None))
    return jax.shard_map(body, mesh=mesh, in_specs=in_specs, out_specs=out_specs, check_vma=False)
```

time: 920 us -> 145 us (0.16)
  the two profiles are of different devices: /device:TPU:160 before, /device:TPU:32 now
where the time goes in v1:
time: 145 us; the launch traced here: 144 us
  Pallas kernels  139 us (96%)
  local copies, waits for them, and re-layouts  4.32 us (3%)
    pallas_call x1, Pallas kernels, body(): pl.pallas_call(kernel, out_shape=(jax.ShapeDtypeStruct((PAD, hidden), bf1...  139 us

profile of v1, /device:TPU:32, one launch (start us, length us, event | category | flops | bytes accessed | tf_op | source)
XLA Modules:
  0.0 143.5 jit_solution(4061422404646562922)
XLA Ops:
  0.6 1.8 %pad.4.w = bf16[64,3200]{1,0:T(8,128)(2,1)} pad(bf16[52,3200]{1,0:T(8,128)(2,1)} %bitcast.10, bf16[]{:T(256)} %constant.2.clone.1), padding=0_12x0_0 | pad | bytes 742402 | tf_op jit(solution)/shard_map/jit(_pad)/pad | solution.py:474
  2.4 138.6 %shard_map.86 = (bf16[64,3200]{1,0:T(8,128)(2,1)}, bf16[128,1664]{1,0:T(8,128)(2,1)}) custom-call(bf16[4,32,1664]{2,1,0:T(8,128)(2,1)} %llm.1, s32[4,32]{1,0:T(4,128)} %bitcast.11, s32[1,4]{1,0:T(1,128)} %counts.1, bf16[4,32,1664]{2,1,0:T(8,128)(2,1)} %bitcast.8, bf16[128,3200]{1,0:T(8,128)(2,1)} %bitcast.7, bf16[64,3200]{1,0:T(8,128)(2,1)} %pad.4.w, ...), custom_call_target="tpu_custom_call" | custom-call | tf_op jit(solution)/shard_map/pallas_call | solution.py:506
  141.0 0.0 copy-start
  141.0 1.8 %slice_bitcast_fusion = bf16[1,52,3200]{2,1,0:T(8,128)(2,1)} fusion(bf16[64,3200]{1,0:T(8,128)(2,1)} %get-tuple-element.4), kind=kLoop, calls=%fused_computation | loop fusion | bytes 665600 | tf_op jit(solution)/shard_map/broadcast_in_dim | solution.py:519
  142.8 0.0 copy-done
  142.8 0.8 copy.10
Async XLA Ops:
  141.0 1.8 %copy-start = (bf16[128,1664]{1,0:T(8,128)(2,1)S(1)}, bf16[128,1664]{1,0:T(8,128)(2,1)}, u32[]{:S(2)}) copy-start(bf16[128,1664]{1,0:T(8,128)(2,1)} %get-tuple-element.5) | copy-start | bytes 1277956

commit v2 on v1

--- a/solution.py
+++ b/solution.py
@@ -46,10 +46,10 @@
 def kernel(
     llm, slots, counts, xin, pre, w, scale,
     wout, gout,
-    wx, wg, preb, full, scaled, part, sibs, sibr, rss, rsr, act, slope, agrad,
+    wpad, wx, wg, preb, full, scaled, part, sibs, sibr, rss, rsr, act, slope, agrad,
     dwp, zs, zr, outs, outr, scl, xi, g0f, g0s,
     local_sem, wx_s, wx_r, pre_s, pre_r, sc_s, sc_r, xi_s, xi_r,
-    ag_s, ag_r, sib_s, sib_r, cs_s, cs_r, rs_s, rs_r,
+    ag_s, ag_r, far_s, far_r, sib_s, sib_r, cs_s, cs_r, rs_s, rs_r,
     zag_s, zag_r, zrs_s, zrs_r, out_s, out_r, g0_s, g0_r, g1_s, g1_r,
 ):
     y = lax.axis_index("pipe")
@@ -95,20 +95,33 @@
     loop(1, GROUP, greet)
     for where in (sibling, up_z, down_z):
         pl.semaphore_signal(barrier, inc=1, device_id=where, device_id_type=MESH)
-    pl.semaphore_wait(barrier, GROUP + 2)
-
-    own_w = pltpu.make_async_copy(w.at[:, columns(gid)], wx.at[y * NX + x], local_sem.at[0])
-    own_w.start()
     own_pre = pltpu.make_async_copy(pre.at[:, columns(gid)], preb.at[y * NX + x], local_sem.at[1])
     own_pre.start()
+    wpad[:OWN, :] = w[...]
+    wpad[OWN:, :] = jnp.zeros((PAD - OWN, BLOCKS * LANE), bf16)
+    own_w = pltpu.make_async_copy(wpad.at[:, columns(gid)], wx.at[y * NX + x], local_sem.at[0])
+    own_w.start()
+    scl[y] = scale[...]
+    half_rows = pl.ds(pl.multiple_of(c * HALF, HALF), HALF)
+    row_ids = lax.broadcasted_iota(jnp.int32, (HALF, ROWS), 0) + c * HALF
+    slot_ids = lax.broadcasted_iota(jnp.int32, (HALF, ROWS), 1)
+    for m in range(NY):
+        hit = (slots[m : m + 1, :] == row_ids) & (slot_ids < counts[0, m])
+        onehot = jnp.where(hit, 1.0, 0.0).astype(bf16)
+        full[0, x, m, c] = jnp.dot(onehot, llm[m], preferred_element_type=f32).astype(bf16)
+    for b, s in ((0, 2), (1, 0)):
+
+        @pl.when(y == s)
+        def _():
+            xi[b] = xin[y, half_rows, :]
+
+    pl.semaphore_wait(barrier, GROUP + 2)
 
     def send_w(k):
         p = other(k)
-        remote(w.at[:, columns(p)], wx.at[y * NX + x], wx_s, wx_r, place(p)).start()
+        remote(wpad.at[:, columns(p)], wx.at[y * NX + x], wx_s, wx_r, place(p)).start()
 
     loop(1, GROUP, send_w)
-
-    scl[y] = scale[...]
 
     def send_scale(k):
         py = lax.rem(y + k, NY)
@@ -116,43 +129,113 @@
 
     loop(1, NY, send_scale)
 
-    slot_line = slots[pl.ds(y, 1), :]
-    row_ids = lax.broadcasted_iota(jnp.int32, (HALF, ROWS), 0) + c * HALF
-    slot_ids = lax.broadcasted_iota(jnp.int32, (HALF, ROWS), 1)
-    hit = (slot_line == row_ids) & (slot_ids < counts[0, y])
-    onehot = jnp.where(hit, 1.0, 0.0).astype(bf16)
-    full[0, gid, c] = jnp.dot(onehot, llm[y], preferred_element_type=f32).astype(bf16)
+    def near(k):
+        return lax.rem(x + k * (1 - c), NX), lax.rem(y + k * c, NY)
+
+    def far(k):
+        return lax.rem(x + k * c, NX), lax.rem(y + k * (1 - c), NY)
+
+    def spread(i, q):
+        px, py = near(q)
+        piece = full.at[i, px, py, c]
+
+        def send(k):
+            fx, fy = far(k)
+            remote(piece, piece, far_s.at[i, k], far_r.at[i, NX - k], (fy, z * NX + fx, c)).start()
+
+        loop(1, NX, send)
 
     def ag_send(i):
+        piece = full.at[i, x, y, c]
+
         def send(k):
-            mine = full.at[i, gid, c]
-            remote(mine, mine, ag_s.at[i], ag_r.at[i], place(other(k))).start()
-
-        loop(1, GROUP, send)
+            px, py = near(k)
+            remote(piece, piece, ag_s.at[i, k], ag_r.at[i, NX - k], (py, z * NX + px, c)).start()
+
+        loop(1, NX, send)
+        spread(i, 0)
+
+    def ag_spread(i):
+        for q in (1, 3, 2):
+            take(full.at[i, 0, 0, 0], ag_r.at[i, q])
+            spread(i, q)
+        give(i, 0)
+
+    def give(i, k):
+        fx, fy = far(k)
+
+        @pl.when(c == 0)
+        def _():
+            four = full.at[i, :, fy, 0]
+            remote(four, four, sib_s.at[i, k], sib_r.at[i, k], sibling).start()
+
+        @pl.when(c == 1)
+        def _():
+            four = full.at[i, fx, :, 1]
+            remote(four, four, sib_s.at[i, k], sib_r.at[i, k], sibling).start()
 
     def ag_forward(i):
-        take(full.at[i, pl.ds(0, GROUP - 1), 0], ag_r.at[i])
-        half = full.at[i, :, c]
-        remote(half, half, sib_s.at[i], sib_r.at[i], sibling).start()
+        for k in (1, 3, 2):
+            take(full.at[i, 0, :, 0], far_r.at[i, k])
+            give(i, k)
 
     def ag_finish(i):
-        take(full.at[i, :, oc], sib_r.at[i])
-
-    ag_send(0)
+        for k in range(NX):
+            take(full.at[i, 0, :, 0], sib_r.at[i, k])
+
+    def top_send():
+        @pl.when(c == 0)
+        def _():
+            piece = full.at[0, x, y, 0]
+
+            def send(k):
+                px, py = near(k)
+                remote(piece, piece, ag_s.at[0, k], ag_r.at[0, NX - k], (py, z * NX + px, c)).start()
+
+            loop(1, NX, send)
+
+        @pl.when(c == 1)
+        def _():
+            four = full.at[0, x, :, 1]
+
+            def send(k):
+                fx, fy = far(k)
+                remote(four, four, far_s.at[0, k], far_r.at[0, NX - k], (fy, z * NX + fx, c)).start()
+
+            loop(1, NX, send)
+            give(0, 0)
+
+    def top_spread():
+        @pl.when(c == 0)
+        def _():
+            for q in (1, 3, 2):
+                take(full.at[0, 0, 0, 0], ag_r.at[0, q])
+                spread(0, q)
+            give(0, 0)
+
+    def top_forward():
+        for k in (1, 3, 2):
+
+            @pl.when(c == 0)
+            def _():
+                take(full.at[0, 0, pl.ds(0, 3), 0], far_r.at[0, k])
+
+            @pl.when(c == 1)
+            def _():
+                take(full.at[0, 0, :, 0], far_r.at[0, k])
+
+            give(0, k)
+
+    top_send()
 
     def send_pre(k):
         p = other(k)
         remote(pre.at[:, columns(p)], preb.at[y * NX + x], pre_s, pre_r, place(p)).start()
 
-    loop(1, GROUP, send_pre)
-
-    half_rows = pl.ds(pl.multiple_of(c * HALF, HALF), HALF)
     for b, s in ((0, 2), (1, 0)):
 
         @pl.when(y == s)
         def _():
-            xi[b] = xin[y, half_rows, :]
-
             def send(k):
                 py = lax.rem(y + k, NY)
                 remote(xin.at[py, half_rows, :], xi.at[b], xi_s.at[b], xi_r.at[b], (py, dp, c)).start()
@@ -236,6 +319,8 @@
     zag(3, 1)
     pack(2)
     zag(2, 1)
+    top_spread()
+    loop(1, GROUP, send_pre)
     pack(1)
     pack(0)
 
@@ -254,18 +339,18 @@
             take(xi.at[b], xi_r.at[b])
 
         unit, inv_std = unit_rows(b)
-        full[1 + 2 * b, gid, c] = (unit * scl[s]).astype(bf16)
+        full[1 + 2 * b, x, y, c] = (unit * scl[s]).astype(bf16)
 
     ag_send(1)
     zag(3, 2)
     zag(2, 2)
-    ag_forward(0)
+    top_forward()
     zag(3, 3)
     zag(2, 3)
 
     def scale_rows(i, s):
         def one(p):
-            rows = full[2 * i, p].astype(f32) * scl[s]
+            rows = full[2 * i, lax.div(p, NY), lax.rem(p, NY)].astype(f32) * scl[s]
             scaled[i, p] = rows.astype(bf16)
 
         loop(0, GROUP, one)
@@ -305,24 +390,28 @@
             rows = agrad[b, pl.ds(t * WIDE, WIDE), :]
             rows = jnp.where(keep, rows, jnp.zeros_like(rows))
             product = lax.dot_general(rows, weight, (((1,), (1,)), ((), ())), preferred_element_type=f32)
-            part[t * 8 : t * 8 + 8] = product.reshape(8, 2, HALF, D)
-
-    def rs_start(b):
-        def one(p):
-            sibs[b, p] = part[p, oc].astype(bf16)
-
-        loop(0, GROUP, one)
-        remote(sibs.at[b], sibr.at[b], cs_s.at[b], cs_r.at[b], sibling).start()
+            eight = pl.ds(t * 8, 8)
+            part[eight] = product.reshape(8, 2, HALF, D)
+
+            def one(p):
+                sibs[b, p] = part[p, oc].astype(bf16)
+
+            loop(t * 8, t * 8 + 8, one)
+            remote(sibs.at[b, eight], sibr.at[b, eight], cs_s.at[b, t], cs_r.at[b, t], sibling).start()
 
     def rs_middle(b):
-        take(sibr.at[b], cs_r.at[b])
-
-        def one(k):
-            p = other(k)
-            rss[b, p] = (part[p, c] + sibr[b, p].astype(f32)).astype(bf16)
-            remote(rss.at[b, p], rsr.at[b, gid], rs_s.at[b], rs_r.at[b], place(p)).start()
-
-        loop(1, GROUP, one)
+        for t in range(2):
+            take(sibr.at[b, pl.ds(t * 8, 8)], cs_r.at[b, t])
+
+            def one(k):
+                p = t * 8 + lax.rem(gid + k, 8)
+
+                @pl.when(p != gid)
+                def _():
+                    rss[b, p] = (part[p, c] + sibr[b, p].astype(f32)).astype(bf16)
+                    remote(rss.at[b, p], rsr.at[b, gid], rs_s.at[b], rs_r.at[b], place(p)).start()
+
+            loop(0, 8, one)
 
     def rs_finish(b, s):
         take(rsr.at[b, pl.ds(0, GROUP - 1)], rs_r.at[b])
@@ -339,65 +428,68 @@
             - jnp.mean(back, axis=-1, keepdims=True)
             - unit * jnp.mean(back * unit, axis=-1, keepdims=True)
         )
-        return (full[2 * b, gid, c].astype(f32) + back).astype(bf16)
-
-    def weight_part(s, left_ref, right):
+        return (full[2 * b, x, y, c].astype(f32) + back).astype(bf16)
+
+    def weight_part(s, left_ref, right, lead):
         for low, size in ((0, 512), (512, 512), (1024, 640)):
-            left = left_ref[:, :, :, low : low + size].reshape(TOK, size)
+            left = left_ref[lead + (slice(low, low + size),)].reshape(TOK, size)
             dwp[s, low : low + size, :] = lax.dot_general(
                 left, right, (((0,), (0,)), ((), ())), preferred_element_type=f32
             )
 
+    tokens = (slice(None), slice(None), slice(None))
     zag_take(3, 4)
     hidden_back(0, 3)
     zag(1, 1)
     zag(0, 1)
+    ag_spread(1)
     zag_take(2, 4)
     norm_part(0, 2)
-    rs_start(0)
+    weight_part(3, scaled.at[0], act[0], tokens)
+    rs_middle(0)
+    ag_send(3)
     zag(1, 2)
     zag(0, 2)
-    weight_part(3, scaled.at[0], act[0])
-    rs_middle(0)
     zrs(3, 1)
     ag_forward(1)
+    gelu_rows(1, 1, 0)
+    ag_finish(1)
+    weight_part(2, full.at[1], agrad[0], tokens + (slice(None),))
     zag(1, 3)
     zag(0, 3)
-    gelu_rows(1, 1, 0)
-    full[2, gid, c] = rs_finish(0, 2)
+    zrs(2, 1)
+    ag_spread(3)
+    zrs(3, 2)
+    full[2, x, y, c] = rs_finish(0, 2)
     ag_send(2)
     zag(1, 4)
     zag(0, 4)
-    ag_finish(1)
-    weight_part(2, full.at[1], agrad[0])
-    zrs(2, 1)
-    zrs(3, 2)
-    ag_send(3)
+    zrs(2, 2)
+    ag_spread(2)
+    zrs(3, 3)
+    ag_forward(3)
+    zrs(2, 3)
     ag_forward(2)
-    zrs(3, 3)
-    zrs(2, 2)
+    ag_finish(3)
     ag_finish(2)
     scale_rows(1, 1)
     zag_take(1, 4)
     hidden_back(1, 1)
+    weight_part(0, full.at[3], agrad[1], tokens + (slice(None),))
+    zrs(0, 1)
+    weight_part(1, scaled.at[1], act[1], tokens)
+    zrs(1, 1)
     zag_take(0, 4)
     norm_part(1, 0)
-    rs_start(1)
-    weight_part(1, scaled.at[1], act[1])
-    zrs(1, 1)
     zrs(3, 4)
-    zrs(2, 3)
+    zrs(2, 4)
     rs_middle(1)
-    ag_forward(3)
-    ag_finish(3)
-    weight_part(0, full.at[3], agrad[1])
-    zrs(0, 1)
-    zrs(2, 4)
+    zrs(0, 2)
     zrs(1, 2)
-    zrs(0, 2)
     zrs_finish(3)
+    zrs_finish(2)
+    zrs(0, 3)
     zrs(1, 3)
-    zrs(0, 3)
     last = rs_finish(1, 0)
 
     @pl.when(y == 0)
@@ -409,11 +501,10 @@
         g0s[...] = last
         remote(g0s, g0f.at[y, c], g0_s, g0_r, (0, dp, c)).start()
 
-    zrs_finish(2)
+    zrs(0, 4)
     zrs(1, 4)
-    zrs(0, 4)
+    zrs_finish(0)
     zrs_finish(1)
-    zrs_finish(0)
 
     @pl.when(y == 0)
     def _():
@@ -424,20 +515,18 @@
         gout[...] = g0f[...].reshape(NY * ROWS, D)
         take(half, g1_s)
 
-    own = pl.ds(x * NY, NY)
-
     @pl.when((y == 1) | (y == 2))
     def _():
-        gout[...] = full[2, own].reshape(NY * ROWS, D)
+        gout[...] = full[2, x].reshape(NY * ROWS, D)
 
     @pl.when(y == 3)
     def _():
-        gout[...] = full[0, own].reshape(NY * ROWS, D)
+        gout[...] = full[0, x].reshape(NY * ROWS, D)
 
     take(outr.at[pl.ds(0, GROUP - 1)], out_r)
     for p in range(GROUP):
         low = first_block(p) * LANE
-        wout[:, low : low + WIDE] = outr[p]
+        wout[:, low : low + WIDE] = outr[p, :OWN]
 
     take(wx.at[pl.ds(0, GROUP - 1)], wx_s)
     take(preb.at[pl.ds(0, GROUP - 1)], pre_s)
@@ -446,13 +535,29 @@
 
         @pl.when(y == s)
         def _():
-            take(full.at[0, pl.ds(0, NY - 1), 0], xi_s.at[b])
+            take(full.at[0, 0, pl.ds(0, NY - 1), 0], xi_s.at[b])
 
     for i in range(4):
-        take(full.at[i, pl.ds(0, GROUP - 1), 0], ag_s.at[i])
-        take(full.at[i, :, c], sib_s.at[i])
+        for k in range(1, NX):
+            if i > 0:
+                take(full.at[i, 0, 0, 0], ag_s.at[i, k])
+                take(full.at[i, 0, :, 0], far_s.at[i, k])
+        for k in range(NX):
+            take(full.at[i, 0, :, 0], sib_s.at[i, k])
+    for k in range(1, NX):
+
+        @pl.when(c == 0)
+        def _():
+            take(full.at[0, 0, 0, 0], ag_s.at[0, k])
+            take(full.at[0, 0, pl.ds(0, 3), 0], far_s.at[0, k])
+
+        @pl.when(c == 1)
+        def _():
+            take(full.at[0, 0, :, 0], far_s.at[0, k])
+
     for b in range(2):
-        take(sibs.at[b], cs_s.at[b])
+        for t in range(2):
+            take(sibs.at[b, pl.ds(t * 8, 8)], cs_s.at[b, t])
         take(rss.at[b, pl.ds(0, GROUP - 1)], rs_s.at[b])
     for s in range(SECTIONS):
         for d in range(2):
@@ -471,16 +576,16 @@
 
 def body(llm_grad, slot_row, counts, saved_in, saved_pre, weights, channel_scale):
     hidden = saved_pre.shape[3]
-    padded = jnp.pad(weights[0], ((0, PAD - OWN), (0, 0)))
     pre = saved_pre.reshape(NY * ROWS, hidden)
     vmem = pl.BlockSpec(memory_space=pltpu.VMEM)
     anywhere = pl.BlockSpec(memory_space=pl.ANY)
     dma = pltpu.SemaphoreType.DMA
     scratch = [
+        pltpu.VMEM((PAD, BLOCKS * LANE), bf16),
         pltpu.VMEM((GROUP, PAD, WIDE), bf16),
         pltpu.VMEM((SECTIONS, NZ, PACK, WIDE), bf16),
         pltpu.VMEM((GROUP, NY * ROWS, WIDE), bf16),
-        pltpu.VMEM((4, GROUP, 2, HALF, D), bf16),
+        pltpu.VMEM((4, NX, NY, 2, HALF, D), bf16),
         pltpu.VMEM((2, GROUP, 2, HALF, D), bf16),
         pltpu.VMEM((GROUP, 2, HALF, D), f32),
         pltpu.VMEM((2, GROUP, HALF, D), bf16),
@@ -500,23 +605,23 @@
         pltpu.VMEM((NY, 2, HALF, D), bf16),
         pltpu.VMEM((HALF, D), bf16),
         dma((2,)), dma, dma, dma, dma, dma, dma, dma((2,)), dma((2,)),
-        dma((4,)), dma((4,)), dma((4,)), dma((4,)), dma((2,)), dma((2,)), dma((2,)), dma((2,)),
+        dma((4, 4)), dma((4, 4)), dma((4, 4)), dma((4, 4)), dma((4, 4)), dma((4, 4)), dma((2, 2)), dma((2, 2)), dma((2,)), dma((2,)),
         dma((4, 2, 4)), dma((4, 2, 4)), dma((4, 2, 4)), dma((4, 2, 4)), dma, dma, dma, dma, dma, dma,
     ]
     wout, gout = pl.pallas_call(
         kernel,
         out_shape=(
-            jax.ShapeDtypeStruct((PAD, hidden), bf16),
+            jax.ShapeDtypeStruct((OWN, hidden), bf16),
             jax.ShapeDtypeStruct((NY * ROWS, D), bf16),
         ),
-        in_specs=[vmem, vmem, pl.BlockSpec(memory_space=pltpu.SMEM), vmem, anywhere, anywhere, vmem],
+        in_specs=[vmem, vmem, pl.BlockSpec(memory_space=pltpu.SMEM), vmem, anywhere, vmem, vmem],
         out_specs=(vmem, vmem),
         scratch_shapes=scratch,
         compiler_params=pltpu.CompilerParams(
             collective_id=0, has_side_effects=True, vmem_limit_bytes=60 * 1024 * 1024
         ),
-    )(llm_grad, slot_row[:, 0], counts, saved_in[0], pre, padded, channel_scale)
-    return (wout[None, :OWN], gout.reshape(1, NY, ROWS, D))
+    )(llm_grad, slot_row[:, 0], counts, saved_in[0], pre, weights[0], channel_scale)
+    return (wout[None], gout.reshape(1, NY, ROWS, D))
 
 
 def solution(mesh):

time: 145 us -> 120 us (0.83)
  Pallas kernels: 139 us -> 116 us
  local copies, waits for them, and re-layouts: 4.32 us -> 2.56 us
    pallas_call x1, Pallas kernels: 139 us -> 116 us  [body(): pl.pallas_call(kernel, out_shape=(jax.ShapeDtypeStruct((OWN, hidden), bf1...]
    broadcast_in_dim x1 -> x0, local copies, waits for them, and re-layouts: 1.79 us -> none  [body(): return (wout[None, :OWN], gout.reshape(1, NY, ROWS, D))]
    unnamed x3 -> x4, local copies, waits for them, and re-layouts: 0.76 us -> 2.56 us
    pad x1 -> x0, local copies, waits for them, and re-layouts: 1.77 us -> none  [body(): padded = jnp.pad(weights[0], ((0, PAD - OWN), (0, 0)))]
where the time goes in v2:
time: 120 us; the launch traced here: 119 us
  Pallas kernels  116 us (97%)
  local copies, waits for them, and re-layouts  2.56 us (2%)
    pallas_call x1, Pallas kernels, body(): pl.pallas_call(kernel, out_shape=(jax.ShapeDtypeStruct((OWN, hidden), bf1...  116 us
    unnamed x4, local copies, waits for them, and re-layouts  2.56 us

profile of v2, /device:TPU:32, one launch (start us, length us, event | category | flops | bytes accessed | tf_op | source)
XLA Modules:
  0.0 119.4 jit_solution(14763041462519153805)
XLA Ops:
  0.6 116.2 %shard_map.86 = (bf16[52,3200]{1,0:T(8,128)(2,1)}, bf16[128,1664]{1,0:T(8,128)(2,1)}) custom-call(bf16[4,32,1664]{2,1,0:T(8,128)(2,1)} %llm.1, s32[4,32]{1,0:T(4,128)} %bitcast.11, s32[1,4]{1,0:T(1,128)} %counts.1, bf16[4,32,1664]{2,1,0:T(8,128)(2,1)} %bitcast.7, bf16[128,3200]{1,0:T(8,128)(2,1)} %bitcast.6, bf16[52,3200]{1,0:T(8,128)(2,1)} %bitcast.10, ...), custom_call_target="tpu_custom_call" | custom-call | tf_op jit(solution)/shard_map/pallas_call | solution.py:611
  116.8 0.0 copy-start
  116.9 1.8 %copy.11 = bf16[1,52,3200]{2,1,0:T(8,128)(2,1)} copy(bf16[1,52,3200]{2,1,0:T(8,128)(2,1)} %bitcast.9) | data formatting | bytes 665600
  118.7 0.0 copy-done
  118.7 0.8 copy.12
Async XLA Ops:
  116.8 1.8 %copy-start = (bf16[128,1664]{1,0:T(8,128)(2,1)S(1)}, bf16[128,1664]{1,0:T(8,128)(2,1)}, u32[]{:S(2)}) copy-start(bf16[128,1664]{1,0:T(8,128)(2,1)} %get-tuple-element.5) | copy-start | bytes 1277956

commit v3 on v2

--- a/solution.py
+++ b/solution.py
@@ -84,8 +84,58 @@
     def take(ref, sem):
         pltpu.make_async_copy(ref, ref, sem).wait()
 
-    def columns(piece):
-        return pl.ds(pl.multiple_of(lax.div(23 * piece, 15) * LANE, LANE), WIDE)
+    def is_narrow(piece):
+        return (lax.rem(piece, 2) == 1) & (piece < 14)
+
+    slim = is_narrow(gid)
+    broad = jnp.logical_not(slim)
+    upper = pl.ds(LANE, LANE)
+
+    def put(src, dst, piece, send, recv):
+        low = lax.div(23 * piece, 15) * LANE
+
+        @pl.when(is_narrow(piece))
+        def _():
+            part_src = src.at[:, pl.ds(pl.multiple_of(low + LANE, LANE), LANE)]
+            remote(part_src, dst.at[:, upper], send.at[1], recv, place(piece)).start()
+
+        @pl.when(jnp.logical_not(is_narrow(piece)))
+        def _():
+            part_src = src.at[:, pl.ds(pl.multiple_of(low, LANE), WIDE)]
+            remote(part_src, dst, send.at[0], recv, place(piece)).start()
+
+    def keep_own(src, dst, sem):
+        low = lax.div(23 * gid, 15) * LANE
+
+        @pl.when(slim)
+        def _():
+            part_src = src.at[:, pl.ds(pl.multiple_of(low + LANE, LANE), LANE)]
+            pltpu.make_async_copy(part_src, dst.at[:, upper], sem).start()
+
+        @pl.when(broad)
+        def _():
+            part_src = src.at[:, pl.ds(pl.multiple_of(low, LANE), WIDE)]
+            pltpu.make_async_copy(part_src, dst, sem).start()
+
+    def take_pieces(ref, low, size, sem):
+        @pl.when(slim)
+        def _():
+            take(ref.at[pl.ds(low, size), :, upper], sem)
+
+        @pl.when(broad)
+        def _():
+            take(ref.at[pl.ds(low, size)], sem)
+
+    def take_mixed(ref, sem):
+        @pl.when(slim)
+        def _():
+            take(ref.at[pl.ds(0, 9)], sem.at[0])
+            take(ref.at[pl.ds(0, 6), :, upper], sem.at[1])
+
+        @pl.when(broad)
+        def _():
+            take(ref.at[pl.ds(0, 8)], sem.at[0])
+            take(ref.at[pl.ds(0, 7), :, upper], sem.at[1])
 
     barrier = pltpu.get_barrier_semaphore()
 
@@ -95,12 +145,16 @@
     loop(1, GROUP, greet)
     for where in (sibling, up_z, down_z):
         pl.semaphore_signal(barrier, inc=1, device_id=where, device_id_type=MESH)
-    own_pre = pltpu.make_async_copy(pre.at[:, columns(gid)], preb.at[y * NX + x], local_sem.at[1])
-    own_pre.start()
+    keep_own(pre, preb.at[y * NX + x], local_sem.at[1])
+
+    @pl.when(slim)
+    def _():
+        wx[:, :, :LANE] = jnp.zeros((GROUP, PAD, LANE), bf16)
+        preb[:, :, :LANE] = jnp.zeros((GROUP, NY * ROWS, LANE), bf16)
+
     wpad[:OWN, :] = w[...]
     wpad[OWN:, :] = jnp.zeros((PAD - OWN, BLOCKS * LANE), bf16)
-    own_w = pltpu.make_async_copy(wpad.at[:, columns(gid)], wx.at[y * NX + x], local_sem.at[0])
-    own_w.start()
+    keep_own(wpad, wx.at[y * NX + x], local_sem.at[0])
     scl[y] = scale[...]
     half_rows = pl.ds(pl.multiple_of(c * HALF, HALF), HALF)
     row_ids = lax.broadcasted_iota(jnp.int32, (HALF, ROWS), 0) + c * HALF
@@ -118,8 +172,7 @@
     pl.semaphore_wait(barrier, GROUP + 2)
 
     def send_w(k):
-        p = other(k)
-        remote(wpad.at[:, columns(p)], wx.at[y * NX + x], wx_s, wx_r, place(p)).start()
+        put(wpad, wx.at[y * NX + x], other(k), wx_s, wx_r)
 
     loop(1, GROUP, send_w)
 
@@ -145,7 +198,7 @@
 
         loop(1, NX, send)
 
-    def ag_send(i):
+    def ag_near(i):
         piece = full.at[i, x, y, c]
 
         def send(k):
@@ -153,7 +206,14 @@
             remote(piece, piece, ag_s.at[i, k], ag_r.at[i, NX - k], (py, z * NX + px, c)).start()
 
         loop(1, NX, send)
+
+    def ag_send(i):
+        ag_near(i)
         spread(i, 0)
+
+    def ag_far(i):
+        spread(i, 0)
+        ag_spread(i)
 
     def ag_spread(i):
         for q in (1, 3, 2):
@@ -226,24 +286,20 @@
 
             give(0, k)
 
-    top_send()
-
     def send_pre(k):
-        p = other(k)
-        remote(pre.at[:, columns(p)], preb.at[y * NX + x], pre_s, pre_r, place(p)).start()
-
-    for b, s in ((0, 2), (1, 0)):
-
-        @pl.when(y == s)
-        def _():
-            def send(k):
-                py = lax.rem(y + k, NY)
-                remote(xin.at[py, half_rows, :], xi.at[b], xi_s.at[b], xi_r.at[b], (py, dp, c)).start()
-
-            loop(1, NY, send)
-
-    take(wx.at[pl.ds(0, GROUP - 1)], wx_r)
-    own_w.wait()
+        put(pre, preb.at[y * NX + x], other(k), pre_s, pre_r)
+
+    def rows_send():
+        for b, s in ((0, 2), (1, 0)):
+
+            @pl.when(y == s)
+            def _():
+                def send(k):
+                    py = lax.rem(y + k, NY)
+                    remote(xin.at[py, half_rows, :], xi.at[b], xi_s.at[b], xi_r.at[b], (py, dp, c)).start()
+
+                loop(1, NY, send)
+
     to_row = lax.broadcasted_iota(jnp.int32, (PACK, NX * PAD), 0)
     from_row = lax.broadcasted_iota(jnp.int32, (PACK, NX * PAD), 1)
     from_block = lax.shift_right_logical(from_row, 6)
@@ -309,22 +365,18 @@
             def _():
                 outr[gid] = outs[s * NX + px]
 
-            @pl.when(jnp.logical_not(mine))
-            def _():
-                remote(outs.at[s * NX + px], outr.at[gid], out_s, out_r, (s, z * NX + px, c)).start()
+            where = (s, z * NX + px, c)
+
+            @pl.when(jnp.logical_not(mine) & slim)
+            def _():
+                src, dst = outs.at[s * NX + px, :, upper], outr.at[gid, :, upper]
+                remote(src, dst, out_s, out_r.at[1], where).start()
+
+            @pl.when(jnp.logical_not(mine) & broad)
+            def _():
+                remote(outs.at[s * NX + px], outr.at[gid], out_s, out_r.at[0], where).start()
 
         loop(0, NX, send)
-
-    pack(3)
-    zag(3, 1)
-    pack(2)
-    zag(2, 1)
-    top_spread()
-    loop(1, GROUP, send_pre)
-    pack(1)
-    pack(0)
-
-    take(scl.at[pl.ds(0, NY - 1)], sc_r)
 
     def unit_rows(b):
         values = xi[b].astype(f32)
@@ -332,21 +384,13 @@
         inv_std = lax.rsqrt(jnp.mean(center * center, axis=-1, keepdims=True) + norm_eps)
         return center * inv_std, inv_std
 
-    for b, s in ((0, 2), (1, 0)):
-
+    def norm_rows(b, s):
         @pl.when(y != s)
         def _():
             take(xi.at[b], xi_r.at[b])
 
         unit, inv_std = unit_rows(b)
         full[1 + 2 * b, x, y, c] = (unit * scl[s]).astype(bf16)
-
-    ag_send(1)
-    zag(3, 2)
-    zag(2, 2)
-    top_forward()
-    zag(3, 3)
-    zag(2, 3)
 
     def scale_rows(i, s):
         def one(p):
@@ -355,26 +399,21 @@
 
         loop(0, GROUP, one)
 
-    ag_finish(0)
-    scale_rows(0, 3)
-    zag(3, 4)
-    zag(2, 4)
-
-    def gelu_rows(b, down, up):
+    def value_rows(b, s):
         def one(p):
             rows = pl.ds(pl.multiple_of(lax.rem(p, NY) * ROWS, ROWS), ROWS)
             at = pl.ds(pl.multiple_of(p * ROWS, ROWS), ROWS)
-            act[b, at, :] = gelu_value(preb[down * NX + lax.div(p, NY), rows, :].astype(f32)).astype(bf16)
-            slope[b, at, :] = gelu_slope(preb[up * NX + lax.div(p, NY), rows, :].astype(f32))
+            act[b, at, :] = gelu_value(preb[s * NX + lax.div(p, NY), rows, :].astype(f32)).astype(bf16)
 
         loop(0, GROUP, one)
 
-    take(preb.at[pl.ds(0, GROUP - 1)], pre_r)
-    own_pre.wait()
-    gelu_rows(0, 3, 2)
-
-    repeated = jnp.where((lax.rem(gid, 2) == 1) & (gid < 14), LANE, 0)
-    keep = lax.broadcasted_iota(jnp.int32, (WIDE, WIDE), 1) >= repeated
+    def slope_rows(b, s):
+        def one(p):
+            rows = pl.ds(pl.multiple_of(lax.rem(p, NY) * ROWS, ROWS), ROWS)
+            at = pl.ds(pl.multiple_of(p * ROWS, ROWS), ROWS)
+            slope[b, at, :] = gelu_slope(preb[s * NX + lax.div(p, NY), rows, :].astype(f32))
+
+        loop(0, GROUP, one)
 
     def hidden_back(b, down):
         weight = wg[down].reshape(D, WIDE)
@@ -388,7 +427,6 @@
         weight = wg[up].reshape(D, WIDE)
         for t in range(2):
             rows = agrad[b, pl.ds(t * WIDE, WIDE), :]
-            rows = jnp.where(keep, rows, jnp.zeros_like(rows))
             product = lax.dot_general(rows, weight, (((1,), (1,)), ((), ())), preferred_element_type=f32)
             eight = pl.ds(t * 8, 8)
             part[eight] = product.reshape(8, 2, HALF, D)
@@ -437,137 +475,190 @@
                 left, right, (((0,), (0,)), ((), ())), preferred_element_type=f32
             )
 
+    def last_rows():
+        last = rs_finish(1, 0)
+
+        @pl.when(y == 0)
+        def _():
+            g0f[0, c] = last
+
+        @pl.when(y != 0)
+        def _():
+            g0s[...] = last
+            remote(g0s, g0f.at[y, c], g0_s, g0_r, (0, dp, c)).start()
+
+    def rows_out():
+        @pl.when(y == 0)
+        def _():
+            take(g0f.at[pl.ds(1, NY - 1), 0], g0_r)
+            half = g0f.at[:, c]
+            remote(half, half, g1_s, g1_r, sibling).start()
+            take(g0f.at[:, oc], g1_r)
+            gout[...] = g0f[...].reshape(NY * ROWS, D)
+            take(half, g1_s)
+
+        @pl.when((y == 1) | (y == 2))
+        def _():
+            gout[...] = full[2, x].reshape(NY * ROWS, D)
+
+        @pl.when(y == 3)
+        def _():
+            gout[...] = full[0, x].reshape(NY * ROWS, D)
+
     tokens = (slice(None), slice(None), slice(None))
-    zag_take(3, 4)
-    hidden_back(0, 3)
-    zag(1, 1)
-    zag(0, 1)
-    ag_spread(1)
-    zag_take(2, 4)
-    norm_part(0, 2)
-    weight_part(3, scaled.at[0], act[0], tokens)
-    rs_middle(0)
-    ag_send(3)
-    zag(1, 2)
-    zag(0, 2)
-    zrs(3, 1)
-    ag_forward(1)
-    gelu_rows(1, 1, 0)
-    ag_finish(1)
-    weight_part(2, full.at[1], agrad[0], tokens + (slice(None),))
-    zag(1, 3)
-    zag(0, 3)
-    zrs(2, 1)
-    ag_spread(3)
-    zrs(3, 2)
-    full[2, x, y, c] = rs_finish(0, 2)
-    ag_send(2)
-    zag(1, 4)
-    zag(0, 4)
-    zrs(2, 2)
-    ag_spread(2)
-    zrs(3, 3)
-    ag_forward(3)
-    zrs(2, 3)
-    ag_forward(2)
-    ag_finish(3)
-    ag_finish(2)
-    scale_rows(1, 1)
-    zag_take(1, 4)
-    hidden_back(1, 1)
-    weight_part(0, full.at[3], agrad[1], tokens + (slice(None),))
-    zrs(0, 1)
-    weight_part(1, scaled.at[1], act[1], tokens)
-    zrs(1, 1)
-    zag_take(0, 4)
-    norm_part(1, 0)
-    zrs(3, 4)
-    zrs(2, 4)
-    rs_middle(1)
-    zrs(0, 2)
-    zrs(1, 2)
-    zrs_finish(3)
-    zrs_finish(2)
-    zrs(0, 3)
-    zrs(1, 3)
-    last = rs_finish(1, 0)
-
-    @pl.when(y == 0)
-    def _():
-        g0f[0, c] = last
-
-    @pl.when(y != 0)
-    def _():
-        g0s[...] = last
-        remote(g0s, g0f.at[y, c], g0_s, g0_r, (0, dp, c)).start()
-
-    zrs(0, 4)
-    zrs(1, 4)
-    zrs_finish(0)
-    zrs_finish(1)
-
-    @pl.when(y == 0)
-    def _():
-        take(g0f.at[pl.ds(1, NY - 1), 0], g0_r)
-        half = g0f.at[:, c]
-        remote(half, half, g1_s, g1_r, sibling).start()
-        take(g0f.at[:, oc], g1_r)
-        gout[...] = g0f[...].reshape(NY * ROWS, D)
-        take(half, g1_s)
-
-    @pl.when((y == 1) | (y == 2))
-    def _():
-        gout[...] = full[2, x].reshape(NY * ROWS, D)
-
-    @pl.when(y == 3)
-    def _():
-        gout[...] = full[0, x].reshape(NY * ROWS, D)
-
-    take(outr.at[pl.ds(0, GROUP - 1)], out_r)
-    for p in range(GROUP):
-        low = first_block(p) * LANE
-        wout[:, low : low + WIDE] = outr[p, :OWN]
-
-    take(wx.at[pl.ds(0, GROUP - 1)], wx_s)
-    take(preb.at[pl.ds(0, GROUP - 1)], pre_s)
-    take(scl.at[pl.ds(0, NY - 1)], sc_s)
-    for b, s in ((0, 2), (1, 0)):
-
-        @pl.when(y == s)
-        def _():
-            take(full.at[0, 0, pl.ds(0, NY - 1), 0], xi_s.at[b])
-
-    for i in range(4):
+    every = tokens + (slice(None),)
+
+    def first_drain():
+        take_mixed(wx, wx_s)
+        take_mixed(preb, pre_s)
+        take(scl.at[pl.ds(0, NY - 1)], sc_s)
+        for b, s in ((0, 2), (1, 0)):
+
+            @pl.when(y == s)
+            def _():
+                take(full.at[0, 0, pl.ds(0, NY - 1), 0], xi_s.at[b])
+
+        for i in range(4):
+            for k in range(1, NX):
+                if i > 0:
+                    take(full.at[i, 0, 0, 0], ag_s.at[i, k])
+                    take(full.at[i, 0, :, 0], far_s.at[i, k])
+            for k in range(NX):
+                take(full.at[i, 0, :, 0], sib_s.at[i, k])
         for k in range(1, NX):
-            if i > 0:
-                take(full.at[i, 0, 0, 0], ag_s.at[i, k])
-                take(full.at[i, 0, :, 0], far_s.at[i, k])
-        for k in range(NX):
-            take(full.at[i, 0, :, 0], sib_s.at[i, k])
-    for k in range(1, NX):
-
-        @pl.when(c == 0)
-        def _():
-            take(full.at[0, 0, 0, 0], ag_s.at[0, k])
-            take(full.at[0, 0, pl.ds(0, 3), 0], far_s.at[0, k])
-
-        @pl.when(c == 1)
-        def _():
-            take(full.at[0, 0, :, 0], far_s.at[0, k])
-
-    for b in range(2):
+
+            @pl.when(c == 0)
+            def _():
+                take(full.at[0, 0, 0, 0], ag_s.at[0, k])
+                take(full.at[0, 0, pl.ds(0, 3), 0], far_s.at[0, k])
+
+            @pl.when(c == 1)
+            def _():
+                take(full.at[0, 0, :, 0], far_s.at[0, k])
+
+        for s in range(SECTIONS):
+            for d in range(2):
+                for k in range(1, 5):
+                    take(zag_block(s, 0, d, k), zag_s.at[s, d, k - 1])
+
+    def rs_drain(b):
         for t in range(2):
             take(sibs.at[b, pl.ds(t * 8, 8)], cs_s.at[b, t])
         take(rss.at[b, pl.ds(0, GROUP - 1)], rs_s.at[b])
-    for s in range(SECTIONS):
+
+    def zrs_drain(s):
         for d in range(2):
-            for k in range(1, 5):
-                take(zag_block(s, 0, d, k), zag_s.at[s, d, k - 1])
-                if k == 1:
-                    take(zs.at[s, d, 0, :, pl.ds(d * LANE, LANE)], zrs_s.at[s, d, 0])
-                else:
-                    take(zs.at[s, d, k - 1], zrs_s.at[s, d, k - 1])
-    take(outs.at[pl.ds(0, GROUP - 1)], out_s)
+            take(zs.at[s, d, 0, :, pl.ds(d * LANE, LANE)], zrs_s.at[s, d, 0])
+            for k in range(2, 5):
+                take(zs.at[s, d, k - 1], zrs_s.at[s, d, k - 1])
+
+    def weights_in():
+        take_pieces(wx, 0, GROUP - 1, wx_r)
+        take_pieces(wx, 0, 1, local_sem.at[0])
+
+    def pre_in():
+        take_pieces(preb, 0, GROUP - 1, pre_r)
+        take_pieces(preb, 0, 1, local_sem.at[1])
+
+    top_send()
+    rows_send()
+    weights_in()
+    pack(3)
+    zag(3, 1)
+    pack(2)
+    zag(2, 1)
+    top_spread()
+    loop(1, GROUP, send_pre)
+    pack(1)
+    pack(0)
+    take(scl.at[pl.ds(0, NY - 1)], sc_r)
+    norm_rows(0, 2)
+    norm_rows(1, 0)
+    ag_near(1)
+    ag_near(3)
+    zag(3, 2)
+    zag(2, 2)
+    zag(3, 3)
+    zag(2, 3)
+    zag(1, 1)
+    top_forward()
+    ag_finish(0)
+    scale_rows(0, 3)
+    zag(3, 4)
+    zag(2, 4)
+    zag(0, 1)
+    pre_in()
+    ag_far(1)
+    slope_rows(0, 2)
+    zag_take(3, 4)
+    hidden_back(0, 3)
+    zag_take(2, 4)
+    norm_part(0, 2)
+    zag(1, 2)
+    value_rows(0, 3)
+    weight_part(3, scaled.at[0], act[0], tokens)
+    rs_middle(0)
+    zrs(3, 1)
+    zag(0, 2)
+    value_rows(1, 1)
+    slope_rows(1, 0)
+    ag_forward(1)
+    zag(1, 3)
+    zag(0, 3)
+    ag_finish(1)
+    weight_part(2, full.at[1], agrad[0], every)
+    zrs(2, 1)
+    zrs(3, 2)
+    zag(1, 4)
+    full[2, x, y, c] = rs_finish(0, 2)
+    ag_send(2)
+    ag_far(3)
+    zag(0, 4)
+    ag_spread(2)
+    zrs(3, 3)
+    zrs(2, 2)
+    ag_forward(3)
+    ag_forward(2)
+    ag_finish(2)
+    scale_rows(1, 1)
+    weight_part(1, scaled.at[1], act[1], tokens)
+    zrs(1, 1)
+    zag_take(1, 4)
+    hidden_back(1, 1)
+    zag_take(0, 4)
+    norm_part(1, 0)
+    ag_finish(3)
+    weight_part(0, full.at[3], agrad[1], every)
+    zrs(0, 1)
+    zrs(3, 4)
+    zrs(2, 3)
+    rs_middle(1)
+    zrs(1, 2)
+    zrs(0, 2)
+    zrs(2, 4)
+    zrs_finish(3)
+    first_drain()
+    zrs(1, 3)
+    zrs(0, 3)
+    zrs_finish(2)
+    rs_drain(0)
+    last_rows()
+    zrs(1, 4)
+    zrs(0, 4)
+    zrs_drain(3)
+    zrs_drain(2)
+    rs_drain(1)
+    zrs_finish(1)
+    zrs_finish(0)
+    rows_out()
+    zrs_drain(1)
+    zrs_drain(0)
+    take_mixed(outr, out_r)
+    for p in range(GROUP):
+        skip = LANE if p % 2 == 1 and p < 14 else 0
+        low = first_block(p) * LANE
+        wout[:, low + skip : low + WIDE] = outr[p, :OWN, skip:]
+    take_pieces(outs, 0, GROUP - 1, out_s)
 
     @pl.when(y != 0)
     def _():
@@ -604,9 +695,9 @@
         pltpu.VMEM((2, HALF, D), bf16),
         pltpu.VMEM((NY, 2, HALF, D), bf16),
         pltpu.VMEM((HALF, D), bf16),
-        dma((2,)), dma, dma, dma, dma, dma, dma, dma((2,)), dma((2,)),
+        dma((2,)), dma((2,)), dma, dma((2,)), dma, dma, dma, dma((2,)), dma((2,)),
         dma((4, 4)), dma((4, 4)), dma((4, 4)), dma((4, 4)), dma((4, 4)), dma((4, 4)), dma((2, 2)), dma((2, 2)), dma((2,)), dma((2,)),
-        dma((4, 2, 4)), dma((4, 2, 4)), dma((4, 2, 4)), dma((4, 2, 4)), dma, dma, dma, dma, dma, dma,
+        dma((4, 2, 4)), dma((4, 2, 4)), dma((4, 2, 4)), dma((4, 2, 4)), dma, dma((2,)), dma, dma, dma, dma,
     ]
     wout, gout = pl.pallas_call(
         kernel,

time: 120 us -> 116 us (0.967)
  Pallas kernels: 116 us -> 112 us
    pallas_call x1, Pallas kernels: 116 us -> 112 us  [body(): pl.pallas_call(kernel, out_shape=(jax.ShapeDtypeStruct((OWN, hidden), bf1...]
where the time goes in v3:
time: 116 us; the launch traced here: 115 us
  Pallas kernels  112 us (97%)
  local copies, waits for them, and re-layouts  2.56 us (2%)
    pallas_call x1, Pallas kernels, body(): pl.pallas_call(kernel, out_shape=(jax.ShapeDtypeStruct((OWN, hidden), bf1...  112 us
    unnamed x4, local copies, waits for them, and re-layouts  2.56 us

profile of v3, /device:TPU:32, one launch (start us, length us, event | category | flops | bytes accessed | tf_op | source)
XLA Modules:
  0.0 114.9 jit_solution(15621876248559449766)
XLA Ops:
  0.6 111.7 %shard_map.86 = (bf16[52,3200]{1,0:T(8,128)(2,1)}, bf16[128,1664]{1,0:T(8,128)(2,1)}) custom-call(bf16[4,32,1664]{2,1,0:T(8,128)(2,1)} %llm.1, s32[4,32]{1,0:T(4,128)} %bitcast.11, s32[1,4]{1,0:T(1,128)} %counts.1, bf16[4,32,1664]{2,1,0:T(8,128)(2,1)} %bitcast.7, bf16[128,3200]{1,0:T(8,128)(2,1)} %bitcast.6, bf16[52,3200]{1,0:T(8,128)(2,1)} %bitcast.10, ...), custom_call_target="tpu_custom_call" | custom-call | tf_op jit(solution)/shard_map/pallas_call | solution.py:702
  112.3 0.0 copy-start
  112.3 1.8 %copy.11 = bf16[1,52,3200]{2,1,0:T(8,128)(2,1)} copy(bf16[1,52,3200]{2,1,0:T(8,128)(2,1)} %bitcast.9) | data formatting | bytes 665600
  114.1 0.0 copy-done
  114.1 0.8 copy.12
Async XLA Ops:
  112.3 1.8 %copy-start = (bf16[128,1664]{1,0:T(8,128)(2,1)S(1)}, bf16[128,1664]{1,0:T(8,128)(2,1)}, u32[]{:S(2)}) copy-start(bf16[128,1664]{1,0:T(8,128)(2,1)} %get-tuple-element.5) | copy-start | bytes 1277956

commit v4 on v3

--- a/solution.py
+++ b/solution.py
@@ -46,11 +46,11 @@
 def kernel(
     llm, slots, counts, xin, pre, w, scale,
     wout, gout,
-    wpad, wx, wg, preb, full, scaled, part, sibs, sibr, rss, rsr, act, slope, agrad,
+    wpad, wx, wg, preb, full, scaled, part, wsib, psib, asib, rss, rsr, act, slope, agrad,
     dwp, zs, zr, outs, outr, scl, xi, g0f, g0s,
     local_sem, wx_s, wx_r, pre_s, pre_r, sc_s, sc_r, xi_s, xi_r,
-    ag_s, ag_r, far_s, far_r, sib_s, sib_r, cs_s, cs_r, rs_s, rs_r,
-    zag_s, zag_r, zrs_s, zrs_r, out_s, out_r, g0_s, g0_r, g1_s, g1_r,
+    ag_s, ag_r, far_s, far_r, sib_s, sib_r, ws_s, ws_r, ps_s, ps_r, as_s, as_r, rs_s, rs_r,
+    zag_s, zag_r, zrs_s, zrs_r, out_s, out_r, g0_s, g0_r,
 ):
     y = lax.axis_index("pipe")
     dp = lax.axis_index("dp")
@@ -90,52 +90,55 @@
     slim = is_narrow(gid)
     broad = jnp.logical_not(slim)
     upper = pl.ds(LANE, LANE)
-
-    def put(src, dst, piece, send, recv):
+    one_dim = (slice(None),)
+    tokens = (slice(None), slice(None), slice(None))
+    every = tokens + one_dim
+
+    def put(src, dst, piece, send, recv, lead):
         low = lax.div(23 * piece, 15) * LANE
 
         @pl.when(is_narrow(piece))
         def _():
-            part_src = src.at[:, pl.ds(pl.multiple_of(low + LANE, LANE), LANE)]
-            remote(part_src, dst.at[:, upper], send.at[1], recv, place(piece)).start()
+            part_src = src.at[lead + (pl.ds(pl.multiple_of(low + LANE, LANE), LANE),)]
+            remote(part_src, dst.at[lead + (upper,)], send.at[1], recv, place(piece)).start()
 
         @pl.when(jnp.logical_not(is_narrow(piece)))
         def _():
-            part_src = src.at[:, pl.ds(pl.multiple_of(low, LANE), WIDE)]
+            part_src = src.at[lead + (pl.ds(pl.multiple_of(low, LANE), WIDE),)]
             remote(part_src, dst, send.at[0], recv, place(piece)).start()
 
-    def keep_own(src, dst, sem):
+    def keep_own(src, dst, sem, lead):
         low = lax.div(23 * gid, 15) * LANE
 
         @pl.when(slim)
         def _():
-            part_src = src.at[:, pl.ds(pl.multiple_of(low + LANE, LANE), LANE)]
-            pltpu.make_async_copy(part_src, dst.at[:, upper], sem).start()
+            part_src = src.at[lead + (pl.ds(pl.multiple_of(low + LANE, LANE), LANE),)]
+            pltpu.make_async_copy(part_src, dst.at[lead + (upper,)], sem).start()
 
         @pl.when(broad)
         def _():
-            part_src = src.at[:, pl.ds(pl.multiple_of(low, LANE), WIDE)]
+            part_src = src.at[lead + (pl.ds(pl.multiple_of(low, LANE), WIDE),)]
             pltpu.make_async_copy(part_src, dst, sem).start()
 
-    def take_pieces(ref, low, size, sem):
+    def take_pieces(ref, low, size, sem, lead):
         @pl.when(slim)
         def _():
-            take(ref.at[pl.ds(low, size), :, upper], sem)
+            take(ref.at[(pl.ds(low, size),) + lead + (upper,)], sem)
 
         @pl.when(broad)
         def _():
             take(ref.at[pl.ds(low, size)], sem)
 
-    def take_mixed(ref, sem):
+    def take_mixed(ref, sem, lead):
         @pl.when(slim)
         def _():
             take(ref.at[pl.ds(0, 9)], sem.at[0])
-            take(ref.at[pl.ds(0, 6), :, upper], sem.at[1])
+            take(ref.at[(pl.ds(0, 6),) + lead + (upper,)], sem.at[1])
 
         @pl.when(broad)
         def _():
             take(ref.at[pl.ds(0, 8)], sem.at[0])
-            take(ref.at[pl.ds(0, 7), :, upper], sem.at[1])
+            take(ref.at[(pl.ds(0, 7),) + lead + (upper,)], sem.at[1])
 
     barrier = pltpu.get_barrier_semaphore()
 
@@ -145,16 +148,21 @@
     loop(1, GROUP, greet)
     for where in (sibling, up_z, down_z):
         pl.semaphore_signal(barrier, inc=1, device_id=where, device_id_type=MESH)
-    keep_own(pre, preb.at[y * NX + x], local_sem.at[1])
+    def greet_across(k):
+        where = (lax.rem(y + k, NY), dp, oc)
+        pl.semaphore_signal(barrier, inc=1, device_id=where, device_id_type=MESH)
+
+    loop(1, NY, greet_across)
+    keep_own(pre, preb.at[y * NX + x], local_sem.at[1], tokens)
 
     @pl.when(slim)
     def _():
         wx[:, :, :LANE] = jnp.zeros((GROUP, PAD, LANE), bf16)
-        preb[:, :, :LANE] = jnp.zeros((GROUP, NY * ROWS, LANE), bf16)
+        preb[:, :, :, :, :LANE] = jnp.zeros((GROUP, NY, 2, HALF, LANE), bf16)
 
     wpad[:OWN, :] = w[...]
     wpad[OWN:, :] = jnp.zeros((PAD - OWN, BLOCKS * LANE), bf16)
-    keep_own(wpad, wx.at[y * NX + x], local_sem.at[0])
+    keep_own(wpad, wx.at[y * NX + x], local_sem.at[0], one_dim)
     scl[y] = scale[...]
     half_rows = pl.ds(pl.multiple_of(c * HALF, HALF), HALF)
     row_ids = lax.broadcasted_iota(jnp.int32, (HALF, ROWS), 0) + c * HALF
@@ -169,10 +177,10 @@
         def _():
             xi[b] = xin[y, half_rows, :]
 
-    pl.semaphore_wait(barrier, GROUP + 2)
+    pl.semaphore_wait(barrier, GROUP + NY + 1)
 
     def send_w(k):
-        put(wpad, wx.at[y * NX + x], other(k), wx_s, wx_r)
+        put(wpad, wx.at[y * NX + x], other(k), wx_s, wx_r, one_dim)
 
     loop(1, GROUP, send_w)
 
@@ -287,7 +295,7 @@
             give(0, k)
 
     def send_pre(k):
-        put(pre, preb.at[y * NX + x], other(k), pre_s, pre_r)
+        put(pre, preb.at[y * NX + x], other(k), pre_s, pre_r, tokens)
 
     def rows_send():
         for b, s in ((0, 2), (1, 0)):
@@ -310,6 +318,13 @@
     def pack(s):
         blocks = wx[s * NX : (s + 1) * NX].reshape(NX * PAD, WIDE)
         wg[s, z] = jnp.dot(pick, blocks, preferred_element_type=f32).astype(bf16)
+        show(s, z)
+
+    def show(s, chunk):
+        remote(wg.at[s, chunk], wsib.at[s, chunk], ws_s.at[s], ws_r.at[s], sibling).start()
+
+    def sibling_weight(s):
+        take(wsib.at[s], ws_r.at[s])
 
     def zag_block(s, chunk, d, k):
         if k == 4:
@@ -319,6 +334,8 @@
     def zag_take(s, k):
         for d, chunk in ((0, lax.rem(z - k + NZ, NZ)), (1, lax.rem(z + k, NZ))):
             take(zag_block(s, chunk, d, k), zag_r.at[s, d, k - 1])
+            if k < 4 or d == 1:
+                show(s, chunk)
 
     def zag(s, k):
         if k > 1:
@@ -392,68 +409,61 @@
         unit, inv_std = unit_rows(b)
         full[1 + 2 * b, x, y, c] = (unit * scl[s]).astype(bf16)
 
-    def scale_rows(i, s):
+    def scale_rows(i, s, half):
         def one(p):
-            rows = full[2 * i, lax.div(p, NY), lax.rem(p, NY)].astype(f32) * scl[s]
-            scaled[i, p] = rows.astype(bf16)
+            rows = full[2 * i, lax.div(p, NY), lax.rem(p, NY), half].astype(f32) * scl[s]
+            scaled[i, p, half] = rows.astype(bf16)
 
         loop(0, GROUP, one)
 
     def value_rows(b, s):
         def one(p):
-            rows = pl.ds(pl.multiple_of(lax.rem(p, NY) * ROWS, ROWS), ROWS)
             at = pl.ds(pl.multiple_of(p * ROWS, ROWS), ROWS)
-            act[b, at, :] = gelu_value(preb[s * NX + lax.div(p, NY), rows, :].astype(f32)).astype(bf16)
+            rows = preb[s * NX + lax.div(p, NY), lax.rem(p, NY)].reshape(ROWS, WIDE)
+            act[b, at, :] = gelu_value(rows.astype(f32)).astype(bf16)
 
         loop(0, GROUP, one)
 
     def slope_rows(b, s):
         def one(p):
-            rows = pl.ds(pl.multiple_of(lax.rem(p, NY) * ROWS, ROWS), ROWS)
-            at = pl.ds(pl.multiple_of(p * ROWS, ROWS), ROWS)
-            slope[b, at, :] = gelu_slope(preb[s * NX + lax.div(p, NY), rows, :].astype(f32))
+            at = pl.ds(pl.multiple_of(p * HALF, HALF), HALF)
+            slope[b, 0, at, :] = gelu_slope(preb[s * NX + lax.div(p, NY), lax.rem(p, NY), c].astype(f32))
 
         loop(0, GROUP, one)
+        take(psib.at[b], ps_r.at[b])
+
+        def two(p):
+            at = pl.ds(pl.multiple_of(p * HALF, HALF), HALF)
+            slope[b, 1, at, :] = gelu_slope(psib[b, lax.div(p, NY), lax.rem(p, NY)].astype(f32))
+
+        loop(0, GROUP, two)
 
     def hidden_back(b, down):
-        weight = wg[down].reshape(D, WIDE)
-        for t in range(2):
-            left = scaled[b, t * 8 : t * 8 + 8].reshape(WIDE, D)
-            hidden = jnp.dot(left, weight, preferred_element_type=f32).astype(bf16).astype(f32)
-            at = pl.ds(t * WIDE, WIDE)
-            agrad[b, at, :] = (hidden * slope[b, at, :]).astype(bf16)
+        left = scaled[b, :, c].reshape(WIDE, D)
+        theirs = jnp.dot(left, wsib[down].reshape(D, WIDE), preferred_element_type=f32).astype(bf16)
+        asib[b] = (theirs.astype(f32) * slope[b, 1]).astype(bf16).reshape(GROUP, HALF, WIDE)
+        remote(asib.at[b], agrad.at[b, :, c], as_s.at[b], as_r.at[b], sibling).start()
+        ours = jnp.dot(left, wg[down].reshape(D, WIDE), preferred_element_type=f32).astype(bf16)
+        agrad[b, :, c] = (ours.astype(f32) * slope[b, 0]).astype(bf16).reshape(GROUP, HALF, WIDE)
 
     def norm_part(b, up):
-        weight = wg[up].reshape(D, WIDE)
-        for t in range(2):
-            rows = agrad[b, pl.ds(t * WIDE, WIDE), :]
-            product = lax.dot_general(rows, weight, (((1,), (1,)), ((), ())), preferred_element_type=f32)
-            eight = pl.ds(t * 8, 8)
-            part[eight] = product.reshape(8, 2, HALF, D)
-
-            def one(p):
-                sibs[b, p] = part[p, oc].astype(bf16)
-
-            loop(t * 8, t * 8 + 8, one)
-            remote(sibs.at[b, eight], sibr.at[b, eight], cs_s.at[b, t], cs_r.at[b, t], sibling).start()
-
-    def rs_middle(b):
-        for t in range(2):
-            take(sibr.at[b, pl.ds(t * 8, 8)], cs_r.at[b, t])
-
-            def one(k):
-                p = t * 8 + lax.rem(gid + k, 8)
-
-                @pl.when(p != gid)
-                def _():
-                    rss[b, p] = (part[p, c] + sibr[b, p].astype(f32)).astype(bf16)
-                    remote(rss.at[b, p], rsr.at[b, gid], rs_s.at[b], rs_r.at[b], place(p)).start()
-
-            loop(0, 8, one)
+        dims = (((1,), (1,)), ((), ()))
+        ours = agrad[b, :, c].reshape(WIDE, WIDE)
+        theirs = asib[b].reshape(WIDE, WIDE)
+        product = lax.dot_general(ours, wg[up].reshape(D, WIDE), dims, preferred_element_type=f32)
+        product += lax.dot_general(theirs, wsib[up].reshape(D, WIDE), dims, preferred_element_type=f32)
+        part[...] = product.reshape(GROUP, HALF, D)
+
+        def one(k):
+            p = other(k)
+            rss[b, p] = part[p].astype(bf16)
+            remote(rss.at[b, p], rsr.at[b, gid], rs_s.at[b], rs_r.at[b], place(p)).start()
+
+        loop(1, GROUP, one)
 
     def rs_finish(b, s):
         take(rsr.at[b, pl.ds(0, GROUP - 1)], rs_r.at[b])
-        total = part[gid, c] + sibr[b, gid].astype(f32)
+        total = part[gid]
 
         def add(k, so_far):
             return so_far + rsr[b, other(k)].astype(f32)
@@ -468,6 +478,10 @@
         )
         return (full[2 * b, x, y, c].astype(f32) + back).astype(bf16)
 
+    def gradient_in(b):
+        take(agrad.at[b, :, oc], as_r.at[b])
+        return agrad[b].reshape(TOK, WIDE)
+
     def weight_part(s, left_ref, right, lead):
         for low, size in ((0, 512), (512, 512), (1024, 640)):
             left = left_ref[lead + (slice(low, low + size),)].reshape(TOK, size)
@@ -478,24 +492,22 @@
     def last_rows():
         last = rs_finish(1, 0)
 
+        g0s[...] = last
+        remote(g0s, g0f.at[y * 2 + c], g0_s, g0_r, (0, dp, oc)).start()
+
         @pl.when(y == 0)
         def _():
-            g0f[0, c] = last
+            g0f[c] = last
 
         @pl.when(y != 0)
         def _():
-            g0s[...] = last
-            remote(g0s, g0f.at[y, c], g0_s, g0_r, (0, dp, c)).start()
+            remote(g0s, g0f.at[y * 2 + c], g0_s, g0_r, (0, dp, c)).start()
 
     def rows_out():
         @pl.when(y == 0)
         def _():
-            take(g0f.at[pl.ds(1, NY - 1), 0], g0_r)
-            half = g0f.at[:, c]
-            remote(half, half, g1_s, g1_r, sibling).start()
-            take(g0f.at[:, oc], g1_r)
+            take(g0f.at[pl.ds(0, 7)], g0_r)
             gout[...] = g0f[...].reshape(NY * ROWS, D)
-            take(half, g1_s)
 
         @pl.when((y == 1) | (y == 2))
         def _():
@@ -505,12 +517,9 @@
         def _():
             gout[...] = full[0, x].reshape(NY * ROWS, D)
 
-    tokens = (slice(None), slice(None), slice(None))
-    every = tokens + (slice(None),)
-
     def first_drain():
-        take_mixed(wx, wx_s)
-        take_mixed(preb, pre_s)
+        take_mixed(wx, wx_s, one_dim)
+        take_mixed(preb, pre_s, tokens)
         take(scl.at[pl.ds(0, NY - 1)], sc_s)
         for b, s in ((0, 2), (1, 0)):
 
@@ -537,14 +546,15 @@
                 take(full.at[0, 0, :, 0], far_s.at[0, k])
 
         for s in range(SECTIONS):
+            take(wsib.at[s], ws_s.at[s])
             for d in range(2):
                 for k in range(1, 5):
                     take(zag_block(s, 0, d, k), zag_s.at[s, d, k - 1])
 
     def rs_drain(b):
-        for t in range(2):
-            take(sibs.at[b, pl.ds(t * 8, 8)], cs_s.at[b, t])
         take(rss.at[b, pl.ds(0, GROUP - 1)], rs_s.at[b])
+        take(asib.at[b], as_s.at[b])
+        take(psib.at[b], ps_s.at[b])
 
     def zrs_drain(s):
         for d in range(2):
@@ -553,12 +563,15 @@
                 take(zs.at[s, d, k - 1], zrs_s.at[s, d, k - 1])
 
     def weights_in():
-        take_pieces(wx, 0, GROUP - 1, wx_r)
-        take_pieces(wx, 0, 1, local_sem.at[0])
+        take_pieces(wx, 0, GROUP - 1, wx_r, one_dim)
+        take_pieces(wx, 0, 1, local_sem.at[0], one_dim)
 
     def pre_in():
-        take_pieces(preb, 0, GROUP - 1, pre_r)
-        take_pieces(preb, 0, 1, local_sem.at[1])
+        take_pieces(preb, 0, GROUP - 1, pre_r, tokens)
+        take_pieces(preb, 0, 1, local_sem.at[1], tokens)
+        for b, s in ((0, 2), (1, 0)):
+            block = preb.at[pl.ds(s * NX, NX), :, oc]
+            remote(block, psib.at[b], ps_s.at[b], ps_r.at[b], sibling).start()
 
     top_send()
     rows_send()
@@ -582,8 +595,7 @@
     zag(2, 3)
     zag(1, 1)
     top_forward()
-    ag_finish(0)
-    scale_rows(0, 3)
+    scale_rows(0, 3, c)
     zag(3, 4)
     zag(2, 4)
     zag(0, 1)
@@ -591,13 +603,16 @@
     ag_far(1)
     slope_rows(0, 2)
     zag_take(3, 4)
+    sibling_weight(3)
     hidden_back(0, 3)
     zag_take(2, 4)
+    sibling_weight(2)
     norm_part(0, 2)
     zag(1, 2)
+    ag_finish(0)
+    scale_rows(0, 3, oc)
     value_rows(0, 3)
     weight_part(3, scaled.at[0], act[0], tokens)
-    rs_middle(0)
     zrs(3, 1)
     zag(0, 2)
     value_rows(1, 1)
@@ -606,7 +621,7 @@
     zag(1, 3)
     zag(0, 3)
     ag_finish(1)
-    weight_part(2, full.at[1], agrad[0], every)
+    weight_part(2, full.at[1], gradient_in(0), every)
     zrs(2, 1)
     zrs(3, 2)
     zag(1, 4)
@@ -619,23 +634,25 @@
     zrs(2, 2)
     ag_forward(3)
     ag_forward(2)
+    zrs(3, 4)
+    scale_rows(1, 1, c)
+    zag_take(1, 4)
+    sibling_weight(1)
+    hidden_back(1, 1)
+    zrs(2, 3)
+    zag_take(0, 4)
+    sibling_weight(0)
+    norm_part(1, 0)
     ag_finish(2)
-    scale_rows(1, 1)
+    scale_rows(1, 1, oc)
     weight_part(1, scaled.at[1], act[1], tokens)
     zrs(1, 1)
-    zag_take(1, 4)
-    hidden_back(1, 1)
-    zag_take(0, 4)
-    norm_part(1, 0)
+    zrs(2, 4)
     ag_finish(3)
-    weight_part(0, full.at[3], agrad[1], every)
+    weight_part(0, full.at[3], gradient_in(1), every)
     zrs(0, 1)
-    zrs(3, 4)
-    zrs(2, 3)
-    rs_middle(1)
     zrs(1, 2)
     zrs(0, 2)
-    zrs(2, 4)
     zrs_finish(3)
     first_drain()
     zrs(1, 3)
@@ -653,21 +670,25 @@
     rows_out()
     zrs_drain(1)
     zrs_drain(0)
-    take_mixed(outr, out_r)
+    take_mixed(outr, out_r, one_dim)
     for p in range(GROUP):
         skip = LANE if p % 2 == 1 and p < 14 else 0
         low = first_block(p) * LANE
         wout[:, low + skip : low + WIDE] = outr[p, :OWN, skip:]
-    take_pieces(outs, 0, GROUP - 1, out_s)
+    take_pieces(outs, 0, GROUP - 1, out_s, one_dim)
+
+    @pl.when(y == 0)
+    def _():
+        take(g0s, g0_s)
 
     @pl.when(y != 0)
     def _():
-        take(g0s, g0_s)
+        take(g0f.at[pl.ds(0, 2)], g0_s)
 
 
 def body(llm_grad, slot_row, counts, saved_in, saved_pre, weights, channel_scale):
     hidden = saved_pre.shape[3]
-    pre = saved_pre.reshape(NY * ROWS, hidden)
+    pre = saved_pre.reshape(NY, 2, HALF, hidden)
     vmem = pl.BlockSpec(memory_space=pltpu.VMEM)
     anywhere = pl.BlockSpec(memory_space=pl.ANY)
     dma = pltpu.SemaphoreType.DMA
@@ -675,17 +696,18 @@
         pltpu.VMEM((PAD, BLOCKS * LANE), bf16),
         pltpu.VMEM((GROUP, PAD, WIDE), bf16),
         pltpu.VMEM((SECTIONS, NZ, PACK, WIDE), bf16),
-        pltpu.VMEM((GROUP, NY * ROWS, WIDE), bf16),
+        pltpu.VMEM((GROUP, NY, 2, HALF, WIDE), bf16),
         pltpu.VMEM((4, NX, NY, 2, HALF, D), bf16),
         pltpu.VMEM((2, GROUP, 2, HALF, D), bf16),
-        pltpu.VMEM((GROUP, 2, HALF, D), f32),
-        pltpu.VMEM((2, GROUP, HALF, D), bf16),
-        pltpu.VMEM((2, GROUP, HALF, D), bf16),
+        pltpu.VMEM((GROUP, HALF, D), f32),
+        pltpu.VMEM((SECTIONS, NZ, PACK, WIDE), bf16),
+        pltpu.VMEM((2, NX, NY, HALF, WIDE), bf16),
+        pltpu.VMEM((2, GROUP, HALF, WIDE), bf16),
         pltpu.VMEM((2, GROUP, HALF, D), bf16),
         pltpu.VMEM((2, GROUP, HALF, D), bf16),
         pltpu.VMEM((2, TOK, WIDE), bf16),
-        pltpu.VMEM((2, TOK, WIDE), f32),
-        pltpu.VMEM((2, TOK, WIDE), bf16),
+        pltpu.VMEM((2, 2, WIDE, WIDE), f32),
+        pltpu.VMEM((2, GROUP, 2, HALF, WIDE), bf16),
         pltpu.VMEM((SECTIONS, D, WIDE), f32),
         pltpu.VMEM((SECTIONS, 2, 4, PACK, WIDE), bf16),
         pltpu.VMEM((SECTIONS, 2, 4, PACK, WIDE), bf16),
@@ -693,11 +715,11 @@
         pltpu.VMEM((GROUP, PAD, WIDE), bf16),
         pltpu.VMEM((SECTIONS, 1, D), f32),
         pltpu.VMEM((2, HALF, D), bf16),
-        pltpu.VMEM((NY, 2, HALF, D), bf16),
+        pltpu.VMEM((NY * 2, HALF, D), bf16),
         pltpu.VMEM((HALF, D), bf16),
         dma((2,)), dma((2,)), dma, dma((2,)), dma, dma, dma, dma((2,)), dma((2,)),
-        dma((4, 4)), dma((4, 4)), dma((4, 4)), dma((4, 4)), dma((4, 4)), dma((4, 4)), dma((2, 2)), dma((2, 2)), dma((2,)), dma((2,)),
-        dma((4, 2, 4)), dma((4, 2, 4)), dma((4, 2, 4)), dma((4, 2, 4)), dma, dma((2,)), dma, dma, dma, dma,
+        dma((4, 4)), dma((4, 4)), dma((4, 4)), dma((4, 4)), dma((4, 4)), dma((4, 4)), dma((4,)), dma((4,)), dma((2,)), dma((2,)), dma((2,)), dma((2,)), dma((2,)), dma((2,)),
+        dma((4, 2, 4)), dma((4, 2, 4)), dma((4, 2, 4)), dma((4, 2, 4)), dma, dma((2,)), dma, dma,
     ]
     wout, gout = pl.pallas_call(
         kernel,

time: 116 us -> 111 us (0.957); the launches traced: 115 us -> 111 us
  Pallas kernels: 112 us -> 108 us
    pallas_call x1, Pallas kernels: 112 us -> 108 us  [body(): pl.pallas_call(kernel, out_shape=(jax.ShapeDtypeStruct((OWN, hidden), bf1...]
where the time goes in v4:
time: 111 us
  Pallas kernels  108 us (97%)
  local copies, waits for them, and re-layouts  2.56 us (2%)
    pallas_call x1, Pallas kernels, body(): pl.pallas_call(kernel, out_shape=(jax.ShapeDtypeStruct((OWN, hidden), bf1...  108 us
    unnamed x4, local copies, waits for them, and re-layouts  2.56 us

profile of v4, /device:TPU:32, one launch (start us, length us, event | category | flops | bytes accessed | tf_op | source)
XLA Modules:
  0.0 111.2 jit_solution(1172176178714961496)
XLA Ops:
  0.6 108.0 %shard_map.86 = (bf16[52,3200]{1,0:T(8,128)(2,1)}, bf16[128,1664]{1,0:T(8,128)(2,1)}) custom-call(bf16[4,32,1664]{2,1,0:T(8,128)(2,1)} %llm.1, s32[4,32]{1,0:T(4,128)} %bitcast.11, s32[1,4]{1,0:T(1,128)} %counts.1, bf16[4,32,1664]{2,1,0:T(8,128)(2,1)} %bitcast.7, bf16[4,2,16,3200]{3,2,1,0:T(8,128)(2,1)} %bitcast.6, bf16[52,3200]{1,0:T(8,128)(2,1)} %bitcast.10, ...), custom_call_target="tpu_custom_call" | custom-call | tf_op jit(solution)/shard_map/pallas_call | solution.py:724
  108.6 0.0 copy-start
  108.6 1.8 %copy.11 = bf16[1,52,3200]{2,1,0:T(8,128)(2,1)} copy(bf16[1,52,3200]{2,1,0:T(8,128)(2,1)} %bitcast.9) | data formatting | bytes 665600
  110.4 0.0 copy-done
  110.4 0.8 copy.12
Async XLA Ops:
  108.6 1.8 %copy-start = (bf16[128,1664]{1,0:T(8,128)(2,1)S(1)}, bf16[128,1664]{1,0:T(8,128)(2,1)}, u32[]{:S(2)}) copy-start(bf16[128,1664]{1,0:T(8,128)(2,1)} %get-tuple-element.5) | copy-start | bytes 1277956

commit v5 on v4

--- a/solution.py
+++ b/solution.py
@@ -575,13 +575,13 @@
 
     top_send()
     rows_send()
+    loop(1, GROUP, send_pre)
     weights_in()
     pack(3)
     zag(3, 1)
     pack(2)
     zag(2, 1)
     top_spread()
-    loop(1, GROUP, send_pre)
     pack(1)
     pack(0)
     take(scl.at[pl.ds(0, NY - 1)], sc_r)
@@ -622,24 +622,24 @@
     zag(0, 3)
     ag_finish(1)
     weight_part(2, full.at[1], gradient_in(0), every)
+    full[2, x, y, c] = rs_finish(0, 2)
+    ag_send(2)
     zrs(2, 1)
     zrs(3, 2)
     zag(1, 4)
-    full[2, x, y, c] = rs_finish(0, 2)
-    ag_send(2)
     ag_far(3)
     zag(0, 4)
+    zrs(2, 2)
     ag_spread(2)
     zrs(3, 3)
-    zrs(2, 2)
     ag_forward(3)
     ag_forward(2)
     zrs(3, 4)
+    zrs(2, 3)
     scale_rows(1, 1, c)
     zag_take(1, 4)
     sibling_weight(1)
     hidden_back(1, 1)
-    zrs(2, 3)
     zag_take(0, 4)
     sibling_weight(0)
     norm_part(1, 0)

time: 111 us -> 110 us (level)
    pallas_call x1, Pallas kernels: 108 us -> 107 us  [body(): pl.pallas_call(kernel, out_shape=(jax.ShapeDtypeStruct((OWN, hidden), bf1...]
where the time goes in v5:
time: 110 us
  Pallas kernels  107 us (97%)
  local copies, waits for them, and re-layouts  2.56 us (2%)
    pallas_call x1, Pallas kernels, body(): pl.pallas_call(kernel, out_shape=(jax.ShapeDtypeStruct((OWN, hidden), bf1...  107 us
    unnamed x4, local copies, waits for them, and re-layouts  2.56 us

profile of v5, /device:TPU:32, one launch (start us, length us, event | category | flops | bytes accessed | tf_op | source)
XLA Modules:
  0.0 109.8 jit_solution(1131915501049485112)
XLA Ops:
  0.6 106.6 %shard_map.86 = (bf16[52,3200]{1,0:T(8,128)(2,1)}, bf16[128,1664]{1,0:T(8,128)(2,1)}) custom-call(bf16[4,32,1664]{2,1,0:T(8,128)(2,1)} %llm.1, s32[4,32]{1,0:T(4,128)} %bitcast.11, s32[1,4]{1,0:T(1,128)} %counts.1, bf16[4,32,1664]{2,1,0:T(8,128)(2,1)} %bitcast.7, bf16[4,2,16,3200]{3,2,1,0:T(8,128)(2,1)} %bitcast.6, bf16[52,3200]{1,0:T(8,128)(2,1)} %bitcast.10, ...), custom_call_target="tpu_custom_call" | custom-call | tf_op jit(solution)/shard_map/pallas_call | solution.py:724
  107.3 0.0 copy-start
  107.3 1.8 %copy.11 = bf16[1,52,3200]{2,1,0:T(8,128)(2,1)} copy(bf16[1,52,3200]{2,1,0:T(8,128)(2,1)} %bitcast.9) | data formatting | bytes 665600
  109.1 0.0 copy-done
  109.1 0.8 copy.12
Async XLA Ops:
  107.3 1.8 %copy-start = (bf16[128,1664]{1,0:T(8,128)(2,1)S(1)}, bf16[128,1664]{1,0:T(8,128)(2,1)}, u32[]{:S(2)}) copy-start(bf16[128,1664]{1,0:T(8,128)(2,1)} %get-tuple-element.5) | copy-start | bytes 1277956
